TPU v7x, 256 devices: a whole 4x4x8 slice. The times are simulated.
256 devices in a mesh: dom: 64 (over y_hi, x, z), cls: 4 (over y_lo, core).
Axes of the slice: x: 4, y: 4 (y_hi: 2, y_lo: 2; y = y_hi * 2 + y_lo), z: 8, core: 2. Of those that a mesh axis runs over, the one named last changes fastest.
Arguments:
- particles: bfloat16 [4096, 2, 2048], P('dom'), may hold values from -8 to 8
- offsets: int32 [4096, 2], P('dom'), may hold values from -3 to 3
- ref_maps: bfloat16 [8, 4096, 2, 2048], P('cls', 'dom'), may hold values from -0.15 to 0.15
- inv_sigma2: float32 [2048], replicated, may hold values from 0.3 to 3
- log_prior: float32 [8], P('cls'), may hold values from -1.5 to 0
- orient: int32 [2, 64], P(None, 'dom'), may hold values from 0 to 63
Outputs:
- slice_sums: float32 [2, 8, 64, 2, 2048], P(None, 'cls', 'dom')
- weight_sums: float32 [2, 8, 64], P(None, 'cls', 'dom')
- particle_loglik: float32 [2, 4096], P(None, 'dom')
All inputs are finite; a program needn't handle non-finite values.
Results may differ from a plain program's by a relative error of at most 0.0019.
The roundings to bfloat16 on the way count: a program that leaves them out, or rounds other values in their place, can miss the bound.
Values may be sent and summed in bfloat16 or wider, within the bound.
A program may use at most 128 MiB of HBM per device.

v0:
```python
import math

import jax
import jax.numpy as jnp
from jax import lax
from jax.sharding import PartitionSpec as P

BOX = 256
KYW = 128
FPIX = 2048
ROUNDS = 2


def shift_block(particles, offsets, step_y):
    particle_count = particles.shape[0]
    pixels = jnp.arange(FPIX, dtype=jnp.int32)
    freq_x = pixels // KYW
    freq_y = pixels % KYW - KYW // 2
    step_x = jnp.arange(5, dtype=jnp.int32) - 2
    shift_x = offsets[:, 0:1] + step_x[None, :]
    shift_y = offsets[:, 1:2] + step_y
    phase_turns = jnp.mod(
        shift_x[:, :, None] * freq_x[None, None, :] + shift_y[:, :, None] * freq_y[None, None, :],
        BOX,
    )
    angles = phase_turns.astype(jnp.float32) * (2.0 * math.pi / BOX)
    cosine_part = jnp.cos(angles)
    sine_part = jnp.sin(angles)
    real_part = particles[:, 0, :].astype(jnp.float32)[:, None, :]
    imag_part = particles[:, 1, :].astype(jnp.float32)[:, None, :]
    shifted = jnp.stack(
        [
            real_part * cosine_part + imag_part * sine_part,
            imag_part * cosine_part - real_part * sine_part,
        ],
        axis=2,
    )
    return shifted.astype(jnp.bfloat16).reshape(particle_count * 5, 2 * FPIX)


def score_pass(particles, offsets, weighted, bias_terms):
    particle_count = particles.shape[0]
    columns = weighted.shape[0]
    score_rows = []
    for step_y in range(-2, 3):
        shifted = shift_block(particles, offsets, step_y)
        score_rows.append(
            jnp.dot(shifted, weighted.T, preferred_element_type=jnp.float32).reshape(
                particle_count, 5, columns
            )
        )
    return jnp.stack(score_rows, axis=1) + bias_terms


def back_pass(particles, offsets, posterior):
    particle_count = particles.shape[0]
    columns = posterior.shape[-1]
    accumulated = jnp.zeros((columns, 2 * FPIX), jnp.float32)
    for block_index, step_y in enumerate(range(-2, 3)):
        shifted = shift_block(particles, offsets, step_y)
        post_rows = posterior[:, block_index].reshape(particle_count * 5, columns)
        accumulated = accumulated + jnp.dot(
            post_rows.T, shifted, preferred_element_type=jnp.float32
        )
    return accumulated


def local(particles, offsets, ref_maps, inv_sigma2, log_prior, orient):
    local_classes = ref_maps.shape[0]
    table_rows = ref_maps.shape[1]
    slot_count = orient.shape[1]
    row_width = 2 * FPIX
    flat_maps = ref_maps.reshape(local_classes, table_rows, row_width)
    noise_weight = jnp.concatenate([inv_sigma2, inv_sigma2])
    slice_list = []
    weight_list = []
    loglik_list = []
    for round_index in range(ROUNDS):
        selector = (
            orient[round_index][:, None] == jnp.arange(table_rows, dtype=jnp.int32)[None, :]
        ).astype(jnp.bfloat16)
        gathered = lax.all_gather(
            jnp.einsum(
                "or,krp->kop", selector, flat_maps, preferred_element_type=jnp.float32
            ).astype(jnp.bfloat16),
            "dom",
            axis=1,
            tiled=True,
        )
        values = gathered.astype(jnp.float32)
        weighted = (values * noise_weight).astype(jnp.bfloat16).reshape(-1, row_width)
        energy = 0.5 * jnp.sum(values * values * noise_weight, axis=-1)
        bias_terms = (log_prior[:, None] - energy).reshape(-1)
        logits = score_pass(particles, offsets, weighted, bias_terms)
        local_peak = jnp.max(logits, axis=(1, 2, 3))
        local_total = jnp.sum(jnp.exp(logits - local_peak[:, None, None, None]), axis=(1, 2, 3))
        maximum = lax.pmax(local_peak, "cls")
        partition = lax.psum(local_total * jnp.exp(local_peak - maximum), "cls")
        posterior = (
            jnp.exp(logits - maximum[:, None, None, None]) / partition[:, None, None, None]
        ).astype(jnp.bfloat16)
        loglik_list.append(maximum + jnp.log(partition))
        partial_value = back_pass(particles, offsets, posterior).reshape(
            local_classes, -1, row_width
        )
        counts = jnp.sum(posterior.astype(jnp.float32), axis=(0, 1, 2)).reshape(local_classes, -1)
        whole_sums, whole_weights = lax.psum((partial_value, counts), "dom")
        first_slot = lax.axis_index("dom") * slot_count
        summed = lax.dynamic_slice_in_dim(whole_sums, first_slot, slot_count, 1)
        weights = lax.dynamic_slice_in_dim(whole_weights, first_slot, slot_count, 1)
        slice_list.append(summed.reshape(local_classes, slot_count, 2, FPIX))
        weight_list.append(weights)
    return (
        jnp.stack(slice_list, axis=0),
        jnp.stack(weight_list, axis=0),
        jnp.stack(loglik_list, axis=0),
    )


def solution(mesh):
    return jax.shard_map(
        local,
        mesh=mesh,
        in_specs=(
            P("dom", None, None),
            P("dom", None),
            P("cls", "dom", None, None),
            P(),
            P("cls"),
            P(None, "dom"),
        ),
        out_specs=(P(None, "cls", "dom", None, None), P(None, "cls", "dom"), P(None, "dom")),
        check_vma=False,
    )
```

profile of v0, /device:TPU:8, one launch (start us, length us, event | category | flops | bytes accessed | tf_op | source)
XLA Modules:
  0.0 1009.9 jit_solution(12680428760754572236)
XLA Ops:
  7.2 1.3 fusion.84
  8.5 1.8 reshape.830
  10.4 0.9 fusion.66
  12.0 0.9 fusion.68
  15.1 55.1 %add_convert_fusion = (bf16[64,5,1,2048]{3,0,2,1:T(8,128)(2,1)S(1)}, bf16[64,5,1,2048]{3,0,2,1:T(8,128)(2,1)S(1)}, bf16[64,5,1,2048]{3,0,2,1:T(8,128)(2,1)S(1)},...) fusion(f32[64,2048]{1,0:T(8,128)S(1)} %get-tuple-element.74, ...), kind=kLoop, calls=%fused_computation.59 | loop fusion | flops 72744960 | bytes 16786688 | tf_op jit(solution)/shard_map/convert.2
  70.5 2.7 copy.59
  73.2 2.6 copy.79
  75.8 1.7 copy.73
  77.9 2.7 copy.53
  80.6 2.6 copy.76
  83.2 1.7 copy.70
  85.3 2.9 copy.55
  88.2 2.6 copy.77
  90.8 1.6 copy.71
  92.8 2.7 copy.57
  95.5 2.7 copy.78
  98.2 1.7 copy.72
  100.2 2.7 copy.51
  102.9 2.6 copy.75
  105.5 1.7 copy.69
  107.2 20.6 %all-gather.7.cloned.1.call-done = bf16[2,262144]{1,0:T(2,128)(2,1)} async-done(((bf16[2,4096]{1,0:T(2,128)(2,1)}), bf16[2,262144]{1,0:T(2,128)(2,1)}) %all-gather.7.cloned.1.call-update) | async-done | bytes 1048592 | tf_op jit(solution)/shard_map/all_gather | solution.py:82
  127.9 3.4 convert.56
  131.2 111.3 %all-gather.5.cloned.1.call-done = bf16[2,262144]{1,0:T(2,128)(2,1)} async-done(((bf16[2,4096]{1,0:T(2,128)(2,1)}), bf16[2,262144]{1,0:T(2,128)(2,1)}) %all-gather.5.cloned.1.call-update) | async-done | bytes 1048592 | tf_op jit(solution)/shard_map/all_gather | solution.py:82
  242.6 2.6 convert.57
  245.2 2.9 fusion.35
  248.3 2.7 fusion.50
  251.1 0.8 fusion.55
  251.9 0.9 copy-done.6
  253.6 0.8 fusion.49
  254.5 0.9 copy-done.7
  256.2 0.8 fusion.53
  257.1 0.9 copy-done.8
  258.8 0.8 fusion.47
  259.7 0.9 copy-done.5
  261.4 0.8 fusion.51
  263.4 5.7 all-reduce.3
  269.1 6.7 all-reduce.2
  275.8 1.4 convert_reduce_fusion.1
  282.9 1.0 copy-done.1
  285.4 1.0 copy-done.2
  288.0 1.0 copy-done.3
  290.5 1.0 copy-done
  291.5 2.1 convolution_add_fusion
  293.6 2.1 convolution_add_fusion.4
  295.9 180.5 %all-reduce = (f32[2,64]{1,0:T(2,128)S(1)}, f32[2,64]{1,0:T(2,128)S(1)}) all-reduce(f32[2,64]{1,0:T(2,128)S(1)} %reshape.836, f32[2,64]{1,0:T(2,128)S(1)} %reshape.835), channel_id=1, replica_groups=mesh['dom'=64,'cls'=4] {'dom'}, use_global_device_ids=true, to_apply=%region_15.16 | all-reduce | flops 256 | bytes 2048 | tf_op jit(solution)/shard_map/psum | solution.py:107
  477.9 522.4 %all-reduce.6.cloned.1.call-done = (f32[2,64,4096]{2,1,0:T(8,128)}, f32[2,64,4096]{2,1,0:T(8,128)}) async-done(((f32[2,64,4096]{2,1,0:T(8,128)}, f32[2,64,4096]{2,1,0:T(8,128)}), (f32[2,64,4096]{2,1,0:T(8,128)}, f32[2,64,4096]{2,1,0:T(8,128)})) %all-reduce.6.cloned.1.call-update) | async-done | bytes 4194320 | tf_op jit(solution)/shard_map/psum | solution.py:107
  1000.3 1.1 dynamic-slice_reduce_fusion
  1001.4 1.1 dynamic-slice_reduce_fusion.1
  (109 shorter events, 21.9 us)
Async XLA Ops:
  7.2 6.5 copy-start.18
  7.2 6.5 copy-start.12
  7.2 120.7 %all-gather.7.cloned.1.call-start = ((), (), s32[]{:S(2)}) async-start(), calls=%async_computation.1 | async-start | bytes 1064960 | tf_op jit(solution)/shard_map/all_gather | solution.py:82
  11.9 230.6 %all-gather.5.cloned.1.call-start = ((), (), s32[]{:S(2)}) async-start(), calls=%async_computation | async-start | bytes 1064960 | tf_op jit(solution)/shard_map/all_gather | solution.py:82
  13.5 986.8 %all-reduce.6.cloned.1.call-start = ((), (), s32[]{:S(2)}) async-start(), calls=%async_computation.2 | async-start | bytes 8388608 | tf_op jit(solution)/shard_map/psum | solution.py:107
  105.5 1.7 copy-start.17
  242.6 2.6 copy-start.10
  245.2 2.9 copy-start.19
  248.3 2.7 copy-start.9
  251.1 1.7 copy-start.6
  253.6 1.7 copy-start.7
  256.2 1.7 copy-start.8
  258.8 1.7 copy-start.5
  262.2 0.9 copy-start.11
  277.6 3.8 copy-start.4
  281.2 0.9 copy-start.16
  282.1 1.7 copy-start.1
  282.1 1.7 copy-start.15
  284.6 1.7 copy-start.2
  286.4 0.9 copy-start.14
  287.3 1.7 copy-start.3
  289.8 1.7 copy-start
  291.5 2.1 copy-start.13
Sparse Core Ops, SparseCore 0:
  12.0 115.7 all-gather.6
  131.9 110.5 all-gather.4
  295.8 704.4 all-reduce.5
where the time goes:
time: 1020 us; the launch traced here: 1010 us
  waiting for transfers between devices  654 us (64%)
  blocking collectives  193 us (19%)
  other arithmetic  70.9 us (7%)
  local copies, waits for them, and re-layouts  54.9 us (5%)
  matrix products  22.2 us (2%)
  between operations  14.5 us (1%)
    psum x1, waiting for transfers between devices, local(): whole_sums, whole_weights = lax.psum((partial_value, counts), 'dom')  522 us
    psum x1, blocking collectives, local(): whole_sums, whole_weights = lax.psum((partial_value, counts), 'dom')  181 us
    all_gather x2, waiting for transfers between devices, local(): lax.all_gather(jnp.einsum('or,krp->kop', selector, flat_maps, preferred_e...  132 us
    another operation x1, other arithmetic  55.1 us
    unnamed x45, local copies, waits for them, and re-layouts  21.1 us
  transfers between devices with their start and end apart: 3, of which 3 were waited for; matrix products, arithmetic and copies ran while one was open for 10% of the time, Pallas kernels for 0%

commit v1 on v0

v1 whole, which is shorter than its diff:
```python
import math

import jax
import jax.numpy as jnp
import numpy as np
from jax import lax
from jax.experimental import pallas as pl
from jax.experimental.pallas import tpu as pltpu
from jax.sharding import PartitionSpec as P

MESH = pl.DeviceIdType.MESH
BOX = 256
KYW = 128
FPIX = 2048
XN = 4
ZN = 8
HALF = 32
STEPS = 25
ROWS = 1792
LIVE = 1600
WIDTH = 2 * FPIX + 128
PACK = 1152
GCUT = 640
SUMW = 128 + FPIX
SCUT = 1152
DELTA = (0, -1, 1, -2, 2, -3, 3, -4)
ORDER = (4, -3, 3, -2, 2, -1, 1, 0)


def tables():
    table = np.zeros((17, 8, 128), np.float64)
    for step in (1, 2, 3):
        for kx in range(16):
            turn = 2.0 * math.pi * ((kx * step) % BOX) / BOX
            table[kx, 2 * step - 2] = math.cos(turn)
            table[kx, 2 * step - 1] = math.sin(turn)
        ky = np.arange(KYW) - KYW // 2
        turn = 2.0 * math.pi * ((ky * step) % BOX) / BOX
        table[16, 2 * step - 2] = np.cos(turn)
        table[16, 2 * step - 1] = np.sin(turn)
    return table.astype(np.float32)


def by_offset(offset, row):
    size = jnp.abs(offset)
    cosine = jnp.where(
        size < 0.5, 1.0, jnp.where(size < 1.5, row[0:1], jnp.where(size < 2.5, row[2:3], row[4:5]))
    )
    sine = jnp.where(
        size < 0.5, 0.0, jnp.where(size < 1.5, row[1:2], jnp.where(size < 2.5, row[3:4], row[5:6]))
    )
    return cosine, jnp.where(offset < 0, -sine, sine)


def rotations(real, imag, row):
    result = [None] * 5
    result[2] = (real, imag)
    for step in (1, 2):
        cosine, sine = row[2 * step - 2 : 2 * step - 1], row[2 * step - 1 : 2 * step]
        rc, rs, ic, is_ = real * cosine, real * sine, imag * cosine, imag * sine
        result[2 + step] = (rc + is_, ic - rs)
        result[2 - step] = (rc - is_, ic + rs)
    return result


def kernel(
    orient, prior, noise, table, offsets, particles, maps,
    sums_out, counts_out, loglik_out,
    block, given, gath, pix, offs, base, shifted, weights, logits, post, stats,
    part, sib, outr, llr,
    ax_l, ax_r, ax_f, az_p, az_m, b_p, b_m, bx_l, bx_r, bx_f,
    s_swap, r_swap, s_pix, r_pix, s_st, r_st, s_out, r_out, s_ll, r_ll,
    s_zp, r_zp, s_zm, r_zm, s_xr, r_xr, s_xl, r_xl, s_xf, r_xf, s_sd, r_sd,
    s_y, r_y, s_wp, r_wp, s_wm, r_wm, s_se, r_se,
    s_d2, r_d2, s_al, r_al, s_ar, r_ar, s_af, r_af, s_ap, r_ap, s_am, r_am,
    s_bp, r_bp, s_bm, r_bm, s_bx, r_bx,
):
    dom, cls = lax.axis_index("dom"), lax.axis_index("cls")
    y_hi, x, z = lax.div(dom, 32), lax.rem(lax.div(dom, 8), XN), lax.rem(dom, ZN)
    y_lo, core = lax.div(cls, 2), lax.rem(cls, 2)
    y = y_hi * 2 + y_lo

    def device(yy, cc, xx, zz):
        return ((lax.div(yy, 2) * XN + xx) * ZN + zz, lax.rem(yy, 2) * 2 + cc)

    def xat(d):
        return lax.rem(x + (XN + d), XN)

    def zat(d):
        return lax.rem(z + (ZN + d), ZN)

    def yat(d):
        return lax.rem(y + d, 4)

    x_up, x_down = device(y, core, xat(1), z), device(y, core, xat(-1), z)
    z_up, z_down = device(y, core, x, zat(1)), device(y, core, x, zat(-1))
    sibling = device(y, 1 - core, x, z)
    across = device(yat(2), 1 - core, x, z)
    mate = device(3 - y, core, x, z)
    y_peers = [device(yat(d), core, x, z) for d in (1, 2, 3)]
    foreign = y_hi != core

    def send(src, dst, ssem, rsem, to):
        copy = pltpu.make_async_remote_copy(
            src_ref=src, dst_ref=dst, send_sem=ssem, recv_sem=rsem, device_id=to, device_id_type=MESH
        )
        copy.start()

    def landed(dst, rsem):
        pltpu.make_async_copy(dst, dst, rsem).wait()

    def left(src, ssem):
        pltpu.make_async_copy(src, src, ssem).wait()

    barrier = pltpu.get_barrier_semaphore()
    for other in [x_up, x_down, z_up, z_down, sibling, across] + y_peers:
        pl.semaphore_signal(barrier, inc=1, device_id=other, device_id_type=MESH)

    lane = lax.broadcasted_iota(jnp.int32, (1, 128), 1)
    weight = noise[...]
    for r in range(2):
        for k in range(2):
            picked = maps[k, orient[r, 0]].astype(jnp.float32)
            scaled = picked * weight
            energy = 0.5 * jnp.sum(jnp.sum(scaled * picked, axis=0, keepdims=True), axis=1, keepdims=True)
            bias = prior[k] - energy
            high = bias.astype(jnp.bfloat16).astype(jnp.float32)
            rest = bias - high
            middle = rest.astype(jnp.bfloat16).astype(jnp.float32)
            low = rest - middle
            row = 2 * r + k
            for q in range(4):
                block[q * 4 + row : q * 4 + row + 1, 0:1024] = scaled[
                    q // 2 : q // 2 + 1, (q % 2) * 1024 : (q % 2) * 1024 + 1024
                ]
                block[q * 4 + row : q * 4 + row + 1, 1024:PACK] = jnp.where(
                    lane == 0, high, jnp.where(lane == 1, middle, jnp.where(lane == 2, low, 0.0))
                )
    given[...] = block[...].astype(jnp.bfloat16)

    first = pl.multiple_of(core * HALF, HALF)
    mine = pl.ds(first, HALF)

    @pl.loop(0, 16)
    def _(tile):
        lanes = pl.ds(pl.multiple_of(tile * 128, 128), 128)
        both = particles[mine, :, lanes].astype(jnp.float32)
        pix[y_hi, 0, :, lanes] = both[:, 0, :].astype(jnp.bfloat16)
        pix[y_hi, 1, :, lanes] = both[:, 1, :].astype(jnp.bfloat16)

    both = offsets[mine, :]
    offs[y_hi] = jnp.where(lane == 0, both[:, 0:1], both[:, 1:2])

    pl.semaphore_wait(barrier, 9)

    own = gath.at[core, z, x]

    @pl.when(foreign)
    def _():
        send(given, gath.at[y_hi, z, x], s_swap, r_swap, across)

    @pl.when(jnp.logical_not(foreign))
    def _():
        own[...] = given[...]

    send(pix.at[y_hi], pix.at[y_hi], s_pix.at[0], r_pix.at[0], mate)
    send(offs.at[y_hi], offs.at[y_hi], s_pix.at[1], r_pix.at[1], mate)

    @pl.when(foreign)
    def _():
        landed(own, r_swap)
        left(given, s_swap)

    ca, cb = pl.ds(0, GCUT), pl.ds(GCUT, PACK - GCUT)

    def ga(dz, dx):
        return gath.at[core, zat(dz), xat(dx), :, ca]

    def gb(dz, dx):
        return gath.at[core, zat(dz), xat(dx), :, cb]

    def ga_row(dz, c=None):
        return gath.at[core if c is None else c, zat(dz), :, :, ca]

    def gb_row(dz, c=None):
        return gath.at[core if c is None else c, zat(dz), :, :, cb]

    def zp(s):
        send(ga(1 - s, 0), ga(1 - s, 0), s_zp.at[s - 1], r_zp.at[s - 1], z_up)

    def zm(s):
        send(ga(s - 1, 0), ga(s - 1, 0), s_zm.at[s - 1], r_zm.at[s - 1], z_down)

    def xs(j):
        ref = ga(DELTA[j], 0)
        send(ref, ref, s_xr.at[j], r_xr.at[j], x_up)
        send(ref, ref, s_xl.at[j], r_xl.at[j], x_down)

    def wait_zp(s):
        landed(ga(-s, 0), r_zp.at[s - 1])

    def wait_zm(s):
        landed(ga(s, 0), r_zm.at[s - 1])

    def far(j):
        landed(ga(DELTA[j], -1), r_xr.at[j])
        if j % 2 == 0:
            ref = ga(DELTA[j], -1)
            send(ref, ref, s_xf.at[j], r_xf.at[j], x_up)
        landed(ga(DELTA[j], 1), r_xl.at[j])
        if j % 2 == 1:
            ref = ga(DELTA[j], 1)
            send(ref, ref, s_xf.at[j], r_xf.at[j], x_down)

    def row_a(j):
        landed(ga(DELTA[j], 2), r_xf.at[j])
        send(ga_row(DELTA[j]), ga_row(DELTA[j]), s_sd.at[j], r_sd.at[j], sibling)

    def wp(s):
        send(gb_row(1 - s), gb_row(1 - s), s_wp.at[s - 1], r_wp.at[s - 1], z_up)

    def wm(s):
        send(gb_row(s - 1), gb_row(s - 1), s_wm.at[s - 1], r_wm.at[s - 1], z_down)

    def row_b(j):
        send(gb_row(DELTA[j]), gb_row(DELTA[j]), s_se.at[j], r_se.at[j], sibling)

    def wait_wp(s):
        landed(gb_row(-s), r_wp.at[s - 1])

    def wait_wm(s):
        landed(gb_row(s), r_wm.at[s - 1])

    def prepare(h):
        both = offs[h].astype(jnp.float32)
        base[0] = jnp.broadcast_to(both[:, 0:1], (HALF, 128))
        cosine, sine = by_offset(jnp.broadcast_to(both[:, 1:2], (HALF, 128)), table[16])
        base[1] = cosine
        base[2] = sine

    def shift(h, begin, end):
        @pl.loop(begin, end)
        def _(kx):
            start = pl.multiple_of(kx * 128, 128)
            row = table[kx]
            for g in range(0, HALF, 16):
                real = pix[h, 0, g : g + 16, pl.ds(start, 128)].astype(jnp.float32)
                imag = pix[h, 1, g : g + 16, pl.ds(start, 128)].astype(jnp.float32)
                cx, sx = by_offset(base[0, g : g + 16], row)
                cy, sy = base[1, g : g + 16], base[2, g : g + 16]
                cosine, sine = cx * cy - sx * sy, sx * cy + cx * sy
                real, imag = real * cosine + imag * sine, imag * cosine - real * sine
                for iy, (ry, iy_) in enumerate(rotations(real, imag, table[16])):
                    for ix, (rx, im) in enumerate(rotations(ry, iy_, row)):
                        at = pl.ds(pl.multiple_of((iy * 5 + ix) * 64 + g + h * HALF, 16), 16)
                        shifted[at, pl.ds(start, 128)] = rx.astype(jnp.bfloat16)
                        shifted[at, pl.ds(pl.multiple_of(start + FPIX, 128), 128)] = im.astype(jnp.bfloat16)

    zp(1)
    zm(1)
    send(gb(0, 0), gb(0, 0), s_y.at[0], r_y.at[0], x_up)
    send(gb(0, 0), gb(0, 0), s_y.at[1], r_y.at[1], x_down)
    xs(0)
    prepare(y_hi)
    shift(y_hi, 0, 2)
    landed(gb(0, -1), r_y.at[0])
    send(gb(0, -1), gb(0, -1), s_y.at[2], r_y.at[2], x_up)
    wait_zp(1)
    zp(2)
    xs(1)
    wait_zm(1)
    zm(2)
    xs(2)
    landed(gb(0, 1), r_y.at[1])
    far(0)
    shift(y_hi, 2, 4)
    landed(gb(0, 2), r_y.at[2])
    wp(1)
    wm(1)
    row_b(0)
    wait_zp(2)
    zp(3)
    xs(3)
    wait_zm(2)
    zm(3)
    xs(4)
    shift(y_hi, 4, 6)
    far(1)
    row_a(0)
    wait_wp(1)
    wp(2)
    wait_wm(1)
    wm(2)
    far(2)
    shift(y_hi, 6, 8)
    wait_zp(3)
    zp(4)
    xs(5)
    wait_zm(3)
    xs(6)
    row_b(1)
    row_b(2)
    row_a(1)
    shift(y_hi, 8, 10)
    wait_wp(2)
    wp(3)
    wait_wm(2)
    wm(3)
    far(3)
    far(4)
    wait_zp(4)
    xs(7)
    row_b(3)
    row_b(4)
    row_a(2)
    shift(y_hi, 10, 12)
    far(5)
    wait_wm(3)
    wm(4)
    wait_wp(3)
    row_b(6)
    row_b(5)
    row_a(3)
    far(6)
    shift(y_hi, 12, 14)
    row_a(4)
    far(7)
    row_a(5)
    shift(y_hi, 14, 16)
    row_a(6)
    row_a(7)

    wide = lax.broadcasted_iota(jnp.int32, (LIVE, 128), 1)
    shifted[0:LIVE, 2 * FPIX : WIDTH] = jnp.where(wide < 3, 1.0, 0.0).astype(jnp.bfloat16)
    shifted[LIVE:ROWS, :] = jnp.zeros((ROWS - LIVE, WIDTH), jnp.bfloat16)
    post[:, LIVE + 64 : ROWS] = jnp.zeros((256, ROWS - LIVE - 64), jnp.bfloat16)

    landed(pix.at[1 - y_hi], r_pix.at[0])
    landed(offs.at[1 - y_hi], r_pix.at[1])
    prepare(1 - y_hi)
    shift(1 - y_hi, 0, 16)

    wait_wm(4)
    row_b(7)
    for j in range(8):
        landed(ga_row(DELTA[j], 1 - core), r_sd.at[j])
        landed(gb_row(DELTA[j], 1 - core), r_se.at[j])

    upper = lax.broadcasted_iota(jnp.int32, (8, 1024), 0) < 4

    @pl.loop(0, 16)
    def _(group):
        gb_, gz = lax.div(group, 8), lax.rem(group, 8)
        rows = pl.ds(pl.multiple_of(group * 16, 16), 16)
        tiles = [gath[gb_, gz, i].astype(jnp.float32) for i in range(4)]
        for t in range(2):
            t0, t1, t2, t3 = [tile[8 * t : 8 * t + 8, 0:1024] for tile in tiles]
            weights[rows, 2048 * t : 2048 * t + 1024] = jnp.concatenate(
                [jnp.where(upper, t0, pltpu.roll(t1, 4, 0)), jnp.where(upper, t2, pltpu.roll(t3, 4, 0))], axis=0
            ).astype(jnp.bfloat16)
            weights[rows, 2048 * t + 1024 : 2048 * t + 2048] = jnp.concatenate(
                [jnp.where(upper, pltpu.roll(t0, 4, 0), t1), jnp.where(upper, pltpu.roll(t2, 4, 0), t3)], axis=0
            ).astype(jnp.bfloat16)
        t0, t1, t2, t3 = [tile[0:8, 1024:PACK] for tile in tiles]
        up = upper[:, 0:128]
        weights[rows, 2 * FPIX : WIDTH] = jnp.concatenate(
            [jnp.where(up, t0, pltpu.roll(t1, 4, 0)), jnp.where(up, t2, pltpu.roll(t3, 4, 0))], axis=0
        ).astype(jnp.bfloat16)

    @pl.loop(0, 7)
    def _(tile):
        at = pl.ds(pl.multiple_of(tile * 256, 256), 256)
        logits[:, at] = lax.dot_general(
            weights[...], shifted[at, :], (((1,), (1,)), ((), ())), preferred_element_type=jnp.float32
        )

    sub = lax.broadcasted_iota(jnp.int32, (8, 128), 0)

    def over_group(value, join):
        value = join(value, pltpu.roll(value, 4, 0))
        value = join(value, jnp.where(sub % 2 == 0, pltpu.roll(value, 7, 0), pltpu.roll(value, 1, 0)))
        return join(value, pltpu.roll(value, 64, 1))

    live = lax.broadcasted_iota(jnp.int32, (256, 128), 1) < 64
    last = pl.ds(LIVE - 64, 128)
    logits[:, last] = jnp.where(live, logits[:, last], -3.0e38)

    def peak_of(tile, carry):
        at = pl.ds(pl.multiple_of(tile * 128, 128), 128)
        return jnp.maximum(carry, jnp.max(logits[:, at].reshape(32, 8, 128), axis=0))

    peak = over_group(lax.fori_loop(0, 13, peak_of, jnp.full((8, 128), -3.0e38, jnp.float32)), jnp.maximum)

    def total_of(tile, carry):
        at = pl.ds(pl.multiple_of(tile * 128, 128), 128)
        value = jnp.exp(logits[:, at].reshape(32, 8, 128) - peak[None])
        logits[:, at] = value.reshape(256, 128)
        return carry + jnp.sum(value, axis=0)

    total = over_group(lax.fori_loop(0, 13, total_of, jnp.zeros((8, 128), jnp.float32)), jnp.add)

    stats[y, 0] = peak
    stats[y, 1] = total
    for i in range(3):
        send(stats.at[y], stats.at[y], s_st.at[i], r_st.at[i], y_peers[i])
    for i in range(3):
        landed(stats.at[yat(3 - i)], r_st.at[i])
    peaks = [stats[i, 0] for i in range(4)]
    top = jnp.maximum(jnp.maximum(peaks[0], peaks[1]), jnp.maximum(peaks[2], peaks[3]))
    whole = stats[0, 1] * jnp.exp(peaks[0] - top)
    for i in range(1, 4):
        whole = whole + stats[i, 1] * jnp.exp(peaks[i] - top)
    scale = jnp.exp(peak - top) / whole
    llr[core] = top + jnp.log(whole)
    send(llr.at[core], llr.at[core], s_ll, r_ll, sibling)

    @pl.loop(0, 13)
    def _(tile):
        at = pl.ds(pl.multiple_of(tile * 128, 128), 128)
        value = logits[:, at].reshape(32, 8, 128) * scale[None]
        post[:, at] = value.reshape(256, 128).astype(jnp.bfloat16)

    def product(at):
        return jnp.dot(post[...], shifted[:, at], preferred_element_type=jnp.float32)

    def store(at, top_, bottom, width):
        keep = lax.broadcasted_iota(jnp.int32, (256, width), 0) % 8 < 4
        even = jnp.where(keep, top_, pltpu.roll(bottom, 4, 0))
        odd = jnp.where(keep, pltpu.roll(top_, 252, 0), bottom)
        part[:, 0, :, at] = even.reshape(32, 8, width)
        part[:, 1, :, at] = odd.reshape(32, 8, width)

    def trade(at, i):
        send(part.at[pl.ds((1 - core) * 16, 16), :, :, at], sib.at[:, :, :, at], s_d2.at[i], r_d2.at[i], sibling)

    def collect(at, i):
        landed(sib.at[:, :, :, at], r_d2.at[i])

        @pl.loop(0, 16)
        def _(pair):
            row = core * 16 + pair
            part[row, :, :, at] = part[row, :, :, at] + sib[pair, :, :, at]

    edge = product(pl.ds(2 * FPIX, 128))
    store(pl.ds(0, 128), edge, edge, 128)
    for j in range(4):
        store(
            pl.ds(128 + 512 * j, 512), product(pl.ds(512 * j, 512)), product(pl.ds(FPIX + 512 * j, 512)), 512
        )
        if j == 1:
            trade(pl.ds(0, SCUT), 0)
        if j == 3:
            trade(pl.ds(SCUT, SUMW - SCUT), 1)

    sa, sb = pl.ds(0, SCUT), pl.ds(SCUT, SUMW - SCUT)

    def pa(dz, dx, at):
        xx = xat(dx)
        return part.at[core * 16 + zat(dz) * 2 + lax.div(xx, 2), lax.rem(xx, 2), :, at]

    def add(dst, src):
        dst[...] = dst[...] + src[...]

    def a_start(i):
        d = ORDER[i]
        if i % 2 == 0:
            send(pa(d, 2, sa), ax_f.at[i], s_af.at[i], r_af.at[i], x_up)
            send(pa(d, -1, sa), ax_r.at[i], s_ar.at[i], r_ar.at[i], x_down)
        else:
            send(pa(d, 2, sa), ax_f.at[i], s_af.at[i], r_af.at[i], x_down)
            send(pa(d, 1, sa), ax_l.at[i], s_al.at[i], r_al.at[i], x_up)

    def a_far(i):
        d = ORDER[i]
        landed(ax_f.at[i], r_af.at[i])
        if i % 2 == 0:
            add(ax_f.at[i], pa(d, 1, sa))
            send(ax_f.at[i], ax_l.at[i], s_al.at[i], r_al.at[i], x_up)
        else:
            add(ax_f.at[i], pa(d, -1, sa))
            send(ax_f.at[i], ax_r.at[i], s_ar.at[i], r_ar.at[i], x_down)

    def a_sum(i):
        own_ = pa(ORDER[i], 0, sa)
        landed(ax_l.at[i], r_al.at[i])
        landed(ax_r.at[i], r_ar.at[i])
        own_[...] = own_[...] + ax_l[i] + ax_r[i]
        if i == 0:
            send(own_, az_p.at[0], s_ap.at[0], r_ap.at[0], z_up)
        elif i == 1:
            send(own_, az_m.at[0], s_am.at[0], r_am.at[0], z_down)
        elif i < 7 and i % 2 == 0:
            s = i // 2
            landed(az_p.at[s - 1], r_ap.at[s - 1])
            add(az_p.at[s - 1], own_)
            send(az_p.at[s - 1], az_p.at[s], s_ap.at[s], r_ap.at[s], z_up)
        elif i < 7:
            s = i // 2
            landed(az_m.at[s - 1], r_am.at[s - 1])
            add(az_m.at[s - 1], own_)
            send(az_m.at[s - 1], az_m.at[s], s_am.at[s], r_am.at[s], z_down)
        else:
            landed(az_p.at[3], r_ap.at[3])
            landed(az_m.at[2], r_am.at[2])
            own_[...] = own_[...] + az_p[3] + az_m[2]

    XREL = (2, 1, -1, 0)

    def b_start(c):
        send(pa(-4, XREL[c], sb), b_m.at[c, 0], s_bm.at[c, 0], r_bm.at[c, 0], z_down)
        send(pa(3, XREL[c], sb), b_p.at[c, 0], s_bp.at[c, 0], r_bp.at[c, 0], z_up)

    def b_step(s, c):
        landed(b_m.at[c, s - 1], r_bm.at[c, s - 1])
        add(b_m.at[c, s - 1], pa(-4 + s, XREL[c], sb))
        send(b_m.at[c, s - 1], b_m.at[c, s], s_bm.at[c, s], r_bm.at[c, s], z_down)
        if s < 3:
            landed(b_p.at[c, s - 1], r_bp.at[c, s - 1])
            add(b_p.at[c, s - 1], pa(3 - s, XREL[c], sb))
            send(b_p.at[c, s - 1], b_p.at[c, s], s_bp.at[c, s], r_bp.at[c, s], z_up)

    def b_sum(c):
        own_ = pa(0, XREL[c], sb)
        landed(b_m.at[c, 3], r_bm.at[c, 3])
        landed(b_p.at[c, 2], r_bp.at[c, 2])
        own_[...] = own_[...] + b_m[c, 3] + b_p[c, 2]
        if c == 0:
            send(own_, bx_f, s_bx.at[0], r_bx.at[0], x_up)
        elif c == 1:
            landed(bx_f, r_bx.at[0])
            add(bx_f, own_)
            send(bx_f, bx_l, s_bx.at[1], r_bx.at[1], x_up)
        elif c == 2:
            send(own_, bx_r, s_bx.at[2], r_bx.at[2], x_down)
        else:
            landed(bx_l, r_bx.at[1])
            landed(bx_r, r_bx.at[2])
            own_[...] = own_[...] + bx_l[...] + bx_r[...]

    collect(pl.ds(0, SCUT), 0)
    for i in range(8):
        a_start(i)
    collect(pl.ds(SCUT, SUMW - SCUT), 1)
    for c in range(4):
        b_start(c)
    a_far(0)
    a_far(1)
    for c in range(4):
        b_step(1, c)
        a_far(2 + c)
    a_sum(0)
    a_sum(1)
    a_far(6)
    b_step(2, 0)
    b_step(2, 1)
    a_far(7)
    b_step(2, 2)
    b_step(2, 3)
    a_sum(2)
    a_sum(3)
    b_step(3, 0)
    b_step(3, 1)
    a_sum(4)
    b_step(3, 2)
    b_step(3, 3)
    a_sum(5)
    b_sum(0)
    b_sum(1)
    a_sum(6)
    b_sum(2)
    b_sum(3)
    a_sum(7)

    done = part.at[core * 16 + z * 2 + lax.div(x, 2), lax.rem(x, 2)]

    @pl.when(foreign)
    def _():
        send(done, outr, s_out, r_out, across)
        left(done, s_out)
        landed(outr, r_out)

    @pl.when(jnp.logical_not(foreign))
    def _():
        outr[...] = done[...]

    counts_out[...] = outr[:, 0:128]
    sums_out[...] = outr[:, 128:SUMW]

    landed(llr.at[1 - core], r_ll)

    loglik_out[...] = jnp.where(
        lax.broadcasted_iota(jnp.int32, (8, 128), 1) < 32,
        jnp.where(y_hi == 0, llr[0], pltpu.roll(llr[0], 96, 1)),
        jnp.where(y_hi == 1, llr[1], pltpu.roll(llr[1], 32, 1)),
    )

    left(pix.at[0], s_pix.at[0])
    left(offs.at[0], s_pix.at[1])
    left(llr.at[0], s_ll)
    for i in range(3):
        left(stats.at[0], s_st.at[i])
        left(gb(0, 0), s_y.at[i])
        left(gb_row(0), s_wp.at[i])
        left(ga(0, 0), s_zm.at[i])
        left(az_m.at[0], s_am.at[i])
        left(bx_f, s_bx.at[i])
    for i in range(4):
        left(gb_row(0), s_wm.at[i])
        left(ga(0, 0), s_zp.at[i])
        left(az_p.at[0], s_ap.at[i])
    for i in range(8):
        left(ga(0, 0), s_xr.at[i])
        left(ga(0, 0), s_xl.at[i])
        left(ga(0, 0), s_xf.at[i])
        left(ga_row(0), s_sd.at[i])
        left(gb_row(0), s_se.at[i])
        left(ax_f.at[0], s_af.at[i])
        left(ax_f.at[0], s_al.at[i])
        left(ax_f.at[0], s_ar.at[i])
    for c in range(4):
        for s in range(4):
            left(b_m.at[0, 0], s_bm.at[c, s])
        for s in range(3):
            left(b_p.at[0, 0], s_bp.at[c, s])
    left(sib.at[:, :, :, sa], s_d2.at[0])
    left(sib.at[:, :, :, sb], s_d2.at[1])


def local(particles, offsets, ref_maps, inv_sigma2, log_prior, orient):
    f32, bf16 = jnp.float32, jnp.bfloat16
    vmem = pl.BlockSpec(memory_space=pltpu.VMEM)
    smem = pl.BlockSpec(memory_space=pltpu.SMEM)
    dma = pltpu.SemaphoreType.DMA

    def twice(*shape):
        return [dma(shape), dma(shape)] if shape else [dma, dma]

    scratch = [
        pltpu.VMEM((16, PACK), f32),
        pltpu.VMEM((16, PACK), bf16),
        pltpu.VMEM((2, ZN, XN, 16, PACK), bf16),
        pltpu.VMEM((2, 2, HALF, FPIX), bf16),
        pltpu.VMEM((2, HALF, 128), jnp.int32),
        pltpu.VMEM((3, HALF, 128), f32),
        pltpu.VMEM((ROWS, WIDTH), bf16),
        pltpu.VMEM((256, WIDTH), bf16),
        pltpu.VMEM((256, ROWS), f32),
        pltpu.VMEM((256, ROWS), bf16),
        pltpu.VMEM((4, 2, 8, 128), f32),
        pltpu.VMEM((32, 2, 8, SUMW), f32),
        pltpu.VMEM((16, 2, 8, SUMW), f32),
        pltpu.VMEM((8, SUMW), f32),
        pltpu.VMEM((2, 8, 128), f32),
        pltpu.VMEM((8, 8, SCUT), f32),
        pltpu.VMEM((8, 8, SCUT), f32),
        pltpu.VMEM((8, 8, SCUT), f32),
        pltpu.VMEM((4, 8, SCUT), f32),
        pltpu.VMEM((3, 8, SCUT), f32),
        pltpu.VMEM((4, 3, 8, SUMW - SCUT), f32),
        pltpu.VMEM((4, 4, 8, SUMW - SCUT), f32),
        pltpu.VMEM((8, SUMW - SCUT), f32),
        pltpu.VMEM((8, SUMW - SCUT), f32),
        pltpu.VMEM((8, SUMW - SCUT), f32),
    ]
    scratch += twice() + twice(2) + twice(3) + twice() + twice()
    scratch += twice(4) + twice(3) + twice(8) * 3 + twice(8)
    scratch += twice(3) + twice(3) + twice(4) + twice(8)
    scratch += twice(2) + twice(8) * 3 + twice(4) + twice(3)
    scratch += twice(4, 3) + twice(4, 4) + twice(3)
    sums, counts, loglik = pl.pallas_call(
        kernel,
        out_shape=(
            jax.ShapeDtypeStruct((8, FPIX), f32),
            jax.ShapeDtypeStruct((8, 128), f32),
            jax.ShapeDtypeStruct((8, 128), f32),
        ),
        in_specs=[smem, smem, vmem, vmem, vmem, vmem, vmem],
        out_specs=(vmem, vmem, vmem),
        scratch_shapes=scratch,
        compiler_params=pltpu.CompilerParams(
            collective_id=0, has_side_effects=True, vmem_limit_bytes=56 * 1024 * 1024
        ),
    )(orient, log_prior, inv_sigma2.reshape(1, FPIX), jnp.asarray(tables()), offsets, particles, ref_maps)
    return (
        sums.reshape(2, 2, 2, FPIX).transpose(1, 2, 0, 3).reshape(2, 2, 1, 2, FPIX),
        counts[0:4, 0].reshape(2, 2, 1),
        jnp.stack([loglik[0, 0:64], loglik[2, 0:64]]),
    )


def solution(mesh):
    return jax.shard_map(
        local,
        mesh=mesh,
        in_specs=(
            P("dom", None, None),
            P("dom", None),
            P("cls", "dom", None, None),
            P(),
            P("cls"),
            P(None, "dom"),
        ),
        out_specs=(P(None, "cls", "dom", None, None), P(None, "cls", "dom"), P(None, "dom")),
        check_vma=False,
    )
```

time: 1020 us -> 91.7 us (0.09)
  the two profiles are of different devices: /device:TPU:8 before, /device:TPU:1 now
where the time goes in v1:
time: 91.7 us; the launch traced here: 91.5 us
  Pallas kernels  85.1 us (93%)
  local copies, waits for them, and re-layouts  5.13 us (6%)
    pallas_call x1, Pallas kernels, local(): pl.pallas_call(kernel, out_shape=(jax.ShapeDtypeStruct((8, FPIX), f32), j...  85.1 us
    unnamed x6, local copies, waits for them, and re-layouts  2.04 us

profile of v1, /device:TPU:1, one launch (start us, length us, event | category | flops | bytes accessed | tf_op | source)
XLA Modules:
  0.0 91.5 jit_solution(3810590640430614764)
XLA Ops:
  0.6 0.0 copy-start.1
  0.6 1.4 %copy.15.offsets = s32[64,2]{1,0:T(8,128)} copy(s32[64,2]{0,1:T(2,128)} %param.8) | data formatting | bytes 1024 | tf_op args[1]
  2.0 0.0 copy-done.1
  2.0 0.6 copy.14.orient
  2.7 85.1 %shard_map.94 = (f32[8,2048]{1,0:T(8,128)}, f32[8,128]{1,0:T(8,128)}, f32[8,128]{1,0:T(8,128)}) custom-call(s32[2,1]{1,0:T(2,128)} %copy.14.orient, f32[2]{0:T(128)} %prior.1, f32[1,2048]{1,0:T(1,128)} %bitcast.8, f32[17,8,128]{2,1,0:T(8,128)} %constant.2.clone.table, s32[64,2]{1,0:T(8,128)} %copy.15.offsets, bf16[64,2,2048]{2,1,0:T(2,128)(2,1)} %particles.1, ...), custom_call_target="tpu_custom_call" | custom-call | tf_op jit(solution)/shard_map/pallas_call | solution.py:670
  87.8 0.8 fusion
  88.6 0.6 pad_maximum_fusion
  89.2 0.9 reshape.16
  90.0 0.0 copy-start
  90.0 0.7 copy.19
  90.7 0.0 copy-done
  90.7 0.1 slice_reduce_fusion
  90.8 0.6 reshape_squeeze.3
Async XLA Ops:
  0.6 1.4 %copy-start.1 = (s32[2,1]{0,1:T(1,128)S(1)}, s32[2,1]{0,1:T(1,128)}, u32[]{:S(2)}) copy-start(s32[2,1]{0,1:T(1,128)} %param.12) | copy-start | bytes 28
  90.0 0.7 copy-start

commit v2 on v1

v2 whole, which is shorter than its diff:
```python
import math

import jax
import jax.numpy as jnp
import numpy as np
from jax import lax
from jax.experimental import pallas as pl
from jax.experimental.pallas import tpu as pltpu
from jax.sharding import PartitionSpec as P

MESH = pl.DeviceIdType.MESH
BOX = 256
KYW = 128
FPIX = 2048
XN = 4
ZN = 8
HALF = 32
STEPS = 25
ROWS = 1792
LIVE = 1600
WIDTH = 2 * FPIX + 128
PACK = 1152
GCUT = 768
SUMW = 128 + FPIX
SCUT = 1664
DELTA = (0, -1, 1, -2, 2, -3, 3, -4)
XPEER = (1, -1, 2)
ZPEER = (1, -1, 2, -2, 3, -3, 4)
ORDER = (4, -3, 3, -2, 2, -1, 1, 0)


def tables():
    table = np.zeros((17, 8, 128), np.float64)
    for step in (1, 2, 3):
        for kx in range(16):
            turn = 2.0 * math.pi * ((kx * step) % BOX) / BOX
            table[kx, 2 * step - 2] = math.cos(turn)
            table[kx, 2 * step - 1] = math.sin(turn)
        ky = np.arange(KYW) - KYW // 2
        turn = 2.0 * math.pi * ((ky * step) % BOX) / BOX
        table[16, 2 * step - 2] = np.cos(turn)
        table[16, 2 * step - 1] = np.sin(turn)
    return table.astype(np.float32)


def by_offset(offset, row):
    size = jnp.abs(offset)
    cosine = jnp.where(
        size < 0.5, 1.0, jnp.where(size < 1.5, row[0:1], jnp.where(size < 2.5, row[2:3], row[4:5]))
    )
    sine = jnp.where(
        size < 0.5, 0.0, jnp.where(size < 1.5, row[1:2], jnp.where(size < 2.5, row[3:4], row[5:6]))
    )
    return cosine, jnp.where(offset < 0, -sine, sine)


def rotations(real, imag, row):
    result = [None] * 5
    result[2] = (real, imag)
    for step in (1, 2):
        cosine, sine = row[2 * step - 2 : 2 * step - 1], row[2 * step - 1 : 2 * step]
        rc, rs, ic, is_ = real * cosine, real * sine, imag * cosine, imag * sine
        result[2 + step] = (rc + is_, ic - rs)
        result[2 - step] = (rc - is_, ic + rs)
    return result


def kernel(
    orient, prior, offsets, noise, table, particles_hbm, maps_hbm,
    sums_out, counts_out, loglik_out,
    particles, maps, block, gath, pix, offs, base, shifted, weights, logits, post, stats,
    part, sib, llr, ax_l, ax_r, ax_f, ae, ag, be, bg, bx,
    s_in, s_pix, r_pix, s_st, r_st, s_ll, r_ll,
    s_z, r_z, s_x, r_x, s_sd, r_sd, s_y, r_y, s_w, r_w, s_se, r_se,
    s_d2, r_d2, s_al, r_al, s_ar, r_ar, s_af, r_af, s_ae, r_ae, s_ag, r_ag,
    s_be, r_be, s_bg, r_bg, s_bx, r_bx,
):
    dom, cls = lax.axis_index("dom"), lax.axis_index("cls")
    y_hi, x, z = lax.div(dom, 32), lax.rem(lax.div(dom, 8), XN), lax.rem(dom, ZN)
    y_lo, core = lax.div(cls, 2), lax.rem(cls, 2)
    y = y_hi * 2 + y_lo

    def device(yy, cc, xx, zz):
        return ((lax.div(yy, 2) * XN + xx) * ZN + zz, lax.rem(yy, 2) * 2 + cc)

    def xat(d):
        return lax.rem(x + (XN + d), XN)

    def zat(d):
        return lax.rem(z + (ZN + d), ZN)

    def yat(d):
        return lax.rem(y + d, 4)

    x_up, x_down = device(y, core, xat(1), z), device(y, core, xat(-1), z)
    sibling = device(y, 1 - core, x, z)
    mate = device(3 - y, core, x, z)
    x_peers = [device(y, core, xat(d), z) for d in XPEER]
    z_peers = [device(y, core, x, zat(d)) for d in ZPEER]
    y_peers = [device(yat(d), core, x, z) for d in (1, 2, 3)]

    def send(src, dst, ssem, rsem, to):
        copy = pltpu.make_async_remote_copy(
            src_ref=src, dst_ref=dst, send_sem=ssem, recv_sem=rsem, device_id=to, device_id_type=MESH
        )
        copy.start()

    def landed(dst, rsem):
        pltpu.make_async_copy(dst, dst, rsem).wait()

    def left(src, ssem):
        pltpu.make_async_copy(src, src, ssem).wait()

    barrier = pltpu.get_barrier_semaphore()
    peers = x_peers + z_peers + y_peers + [sibling]
    for other in peers:
        pl.semaphore_signal(barrier, inc=1, device_id=other, device_id_type=MESH)
    get_maps = pltpu.make_async_copy(maps_hbm, maps, s_in.at[0])
    get_maps.start()
    get_particles = pltpu.make_async_copy(particles_hbm, particles, s_in.at[1])
    get_particles.start()
    get_maps.wait()

    lane = lax.broadcasted_iota(jnp.int32, (1, 128), 1)
    weight = noise[...]
    for r in range(2):
        for k in range(2):
            picked = maps[k, orient[0, r]].astype(jnp.float32)
            scaled = picked * weight
            energy = 0.5 * jnp.sum(jnp.sum(scaled * picked, axis=0, keepdims=True), axis=1, keepdims=True)
            bias = prior[k] - energy
            high = bias.astype(jnp.bfloat16).astype(jnp.float32)
            rest = bias - high
            middle = rest.astype(jnp.bfloat16).astype(jnp.float32)
            low = rest - middle
            row = 2 * r + k
            for q in range(4):
                block[q * 4 + row : q * 4 + row + 1, 0:1024] = scaled[
                    q // 2 : q // 2 + 1, (q % 2) * 1024 : (q % 2) * 1024 + 1024
                ]
                block[q * 4 + row : q * 4 + row + 1, 1024:PACK] = jnp.where(
                    lane == 0, high, jnp.where(lane == 1, middle, jnp.where(lane == 2, low, 0.0))
                )
    gath[core, z, x] = block[...].astype(jnp.bfloat16)
    get_particles.wait()

    first = pl.multiple_of(core * HALF, HALF)
    mine = pl.ds(first, HALF)

    @pl.loop(0, 16)
    def _(tile):
        lanes = pl.ds(pl.multiple_of(tile * 128, 128), 128)
        both = particles[mine, :, lanes].astype(jnp.float32)
        pix[y_hi, 0, :, lanes] = both[:, 0, :].astype(jnp.bfloat16)
        pix[y_hi, 1, :, lanes] = both[:, 1, :].astype(jnp.bfloat16)

    @pl.loop(0, HALF)
    def _(i):
        offs[y_hi, pl.ds(i, 1), :] = jnp.where(lane == 0, offsets[0, first + i], offsets[1, first + i])

    def prepare(h):
        both = offs[h].astype(jnp.float32)
        base[0] = jnp.broadcast_to(both[:, 0:1], (HALF, 128))
        cosine, sine = by_offset(jnp.broadcast_to(both[:, 1:2], (HALF, 128)), table[16])
        base[1] = cosine
        base[2] = sine

    def shift(h, begin, end):
        @pl.loop(begin, end)
        def _(kx):
            start = pl.multiple_of(kx * 128, 128)
            row = table[kx]
            for g in range(0, HALF, 16):
                real = pix[h, 0, g : g + 16, pl.ds(start, 128)].astype(jnp.float32)
                imag = pix[h, 1, g : g + 16, pl.ds(start, 128)].astype(jnp.float32)
                cx, sx = by_offset(base[0, g : g + 16], row)
                cy, sy = base[1, g : g + 16], base[2, g : g + 16]
                cosine, sine = cx * cy - sx * sy, sx * cy + cx * sy
                real, imag = real * cosine + imag * sine, imag * cosine - real * sine
                for iy, (ry, iy_) in enumerate(rotations(real, imag, table[16])):
                    for ix, (rx, im) in enumerate(rotations(ry, iy_, row)):
                        at = pl.ds(pl.multiple_of((iy * 5 + ix) * 64 + g + h * HALF, 16), 16)
                        shifted[at, pl.ds(start, 128)] = rx.astype(jnp.bfloat16)
                        shifted[at, pl.ds(pl.multiple_of(start + FPIX, 128), 128)] = im.astype(jnp.bfloat16)

    prepare(y_hi)
    shift(y_hi, 0, 16)

    wide = lax.broadcasted_iota(jnp.int32, (LIVE, 128), 1)
    shifted[0:LIVE, 2 * FPIX : WIDTH] = jnp.where(wide < 3, 1.0, 0.0).astype(jnp.bfloat16)
    shifted[LIVE:ROWS, :] = jnp.zeros((ROWS - LIVE, WIDTH), jnp.bfloat16)
    post[:, LIVE + 64 : ROWS] = jnp.zeros((256, ROWS - LIVE - 64), jnp.bfloat16)

    pl.semaphore_wait(barrier, len(peers))

    ca, cb = pl.ds(0, GCUT), pl.ds(GCUT, PACK - GCUT)

    def ga(dz, dx):
        return gath.at[core, zat(dz), xat(dx), :, ca]

    def gb(dz, dx):
        return gath.at[core, zat(dz), xat(dx), :, cb]

    def ga_row(dz, c=None):
        return gath.at[core if c is None else c, zat(dz), :, :, ca]

    def gb_row(dz, c=None):
        return gath.at[core if c is None else c, zat(dz), :, :, cb]

    def xs(j):
        ref = ga(DELTA[j], 0)
        for i in range(3):
            send(ref, ref, s_x.at[j, i], r_x.at[j, i], x_peers[i])

    def from_z(j):
        landed(ga(DELTA[j], 0), r_z.at[j - 1])
        xs(j)

    def row_a(j):
        for i in range(3):
            landed(ga(DELTA[j], -XPEER[i]), r_x.at[j, i])
        send(ga_row(DELTA[j]), ga_row(DELTA[j]), s_sd.at[j], r_sd.at[j], sibling)

    def row_b(j):
        send(gb_row(DELTA[j]), gb_row(DELTA[j]), s_se.at[j], r_se.at[j], sibling)

    def w(i, row, step):
        send(gb_row(row), gb_row(row), s_w.at[i], r_w.at[i], device(y, core, x, zat(step)))

    def from_w(i, row, j):
        landed(gb_row(row), r_w.at[i])
        row_b(j)

    for i in range(3):
        send(gb(0, 0), gb(0, 0), s_y.at[i], r_y.at[i], x_peers[i])
    for i in range(7):
        send(ga(0, 0), ga(0, 0), s_z.at[i], r_z.at[i], z_peers[i])
    xs(0)
    send(offs.at[y_hi], offs.at[y_hi], s_pix.at[1], r_pix.at[1], mate)
    send(pix.at[y_hi], pix.at[y_hi], s_pix.at[0], r_pix.at[0], mate)
    for i in range(3):
        landed(gb(0, -XPEER[i]), r_y.at[i])
    for i, step in enumerate((2, -2, 1, -1)):
        w(i, 0, step)
    row_b(0)
    for j in range(1, 5):
        from_z(j)
    row_a(0)
    for j in range(5, 8):
        from_z(j)
    row_a(1)
    from_w(0, -2, 3)
    w(4, -2, 1)
    w(5, -2, 2)
    from_w(1, 2, 4)
    w(6, 2, -1)
    from_w(2, -1, 1)
    from_w(3, 1, 2)
    row_a(2)
    landed(offs.at[1 - y_hi], r_pix.at[1])
    landed(pix.at[1 - y_hi], r_pix.at[0])
    prepare(1 - y_hi)
    shift(1 - y_hi, 0, 6)
    row_a(3)
    row_a(4)
    shift(1 - y_hi, 6, 12)
    row_a(5)
    row_a(6)
    from_w(4, -3, 5)
    from_w(6, 3, 6)
    shift(1 - y_hi, 12, 16)
    from_w(5, -4, 7)
    row_a(7)
    for j in range(8):
        landed(ga_row(DELTA[j], 1 - core), r_sd.at[j])
        landed(gb_row(DELTA[j], 1 - core), r_se.at[j])

    upper = lax.broadcasted_iota(jnp.int32, (8, 1024), 0) < 4

    @pl.loop(0, 16)
    def _(group):
        gb_, gz = lax.div(group, 8), lax.rem(group, 8)
        rows = pl.ds(pl.multiple_of(group * 16, 16), 16)
        tiles = [gath[gb_, gz, i].astype(jnp.float32) for i in range(4)]
        for t in range(2):
            t0, t1, t2, t3 = [tile[8 * t : 8 * t + 8, 0:1024] for tile in tiles]
            weights[rows, 2048 * t : 2048 * t + 1024] = jnp.concatenate(
                [jnp.where(upper, t0, pltpu.roll(t1, 4, 0)), jnp.where(upper, t2, pltpu.roll(t3, 4, 0))], axis=0
            ).astype(jnp.bfloat16)
            weights[rows, 2048 * t + 1024 : 2048 * t + 2048] = jnp.concatenate(
                [jnp.where(upper, pltpu.roll(t0, 4, 0), t1), jnp.where(upper, pltpu.roll(t2, 4, 0), t3)], axis=0
            ).astype(jnp.bfloat16)
        t0, t1, t2, t3 = [tile[0:8, 1024:PACK] for tile in tiles]
        up = upper[:, 0:128]
        weights[rows, 2 * FPIX : WIDTH] = jnp.concatenate(
            [jnp.where(up, t0, pltpu.roll(t1, 4, 0)), jnp.where(up, t2, pltpu.roll(t3, 4, 0))], axis=0
        ).astype(jnp.bfloat16)

    @pl.loop(0, 2)
    def _(tile):
        at = pl.ds(pl.multiple_of(tile * 896, 128), 896)
        logits[:, at] = lax.dot_general(
            shifted[at, :], weights[...], (((1,), (1,)), ((), ())), preferred_element_type=jnp.float32
        ).T

    sub = lax.broadcasted_iota(jnp.int32, (8, 128), 0)

    def over_group(value, join):
        value = join(value, pltpu.roll(value, 4, 0))
        value = join(value, jnp.where(sub % 2 == 0, pltpu.roll(value, 7, 0), pltpu.roll(value, 1, 0)))
        return join(value, pltpu.roll(value, 64, 1))

    live = lax.broadcasted_iota(jnp.int32, (256, 128), 1) < 64
    last = pl.ds(LIVE - 64, 128)
    logits[:, last] = jnp.where(live, logits[:, last], -3.0e38)

    def peak_of(tile, carry):
        at = pl.ds(pl.multiple_of(tile * 128, 128), 128)
        return jnp.maximum(carry, jnp.max(logits[:, at].reshape(32, 8, 128), axis=0))

    peak = over_group(lax.fori_loop(0, 13, peak_of, jnp.full((8, 128), -3.0e38, jnp.float32)), jnp.maximum)

    def total_of(tile, carry):
        at = pl.ds(pl.multiple_of(tile * 128, 128), 128)
        value = jnp.exp(logits[:, at].reshape(32, 8, 128) - peak[None])
        logits[:, at] = value.reshape(256, 128)
        return carry + jnp.sum(value, axis=0)

    total = over_group(lax.fori_loop(0, 13, total_of, jnp.zeros((8, 128), jnp.float32)), jnp.add)

    stats[y, 0] = peak
    stats[y, 1] = total
    for i in range(3):
        send(stats.at[y], stats.at[y], s_st.at[i], r_st.at[i], y_peers[i])
    for i in range(3):
        landed(stats.at[yat(3 - i)], r_st.at[i])
    peaks = [stats[i, 0] for i in range(4)]
    top = jnp.maximum(jnp.maximum(peaks[0], peaks[1]), jnp.maximum(peaks[2], peaks[3]))
    whole = stats[0, 1] * jnp.exp(peaks[0] - top)
    for i in range(1, 4):
        whole = whole + stats[i, 1] * jnp.exp(peaks[i] - top)
    scale = jnp.exp(peak - top) / whole
    llr[core] = top + jnp.log(whole)
    send(llr.at[core], llr.at[core], s_ll, r_ll, sibling)

    @pl.loop(0, 13)
    def _(tile):
        at = pl.ds(pl.multiple_of(tile * 128, 128), 128)
        value = logits[:, at].reshape(32, 8, 128) * scale[None]
        post[:, at] = value.reshape(256, 128).astype(jnp.bfloat16)

    def product(at):
        return jnp.dot(post[...], shifted[:, at], preferred_element_type=jnp.float32)

    def store(at, top_, bottom, width):
        keep = lax.broadcasted_iota(jnp.int32, (256, width), 0) % 8 < 4
        even = jnp.where(keep, top_, pltpu.roll(bottom, 4, 0))
        odd = jnp.where(keep, pltpu.roll(top_, 252, 0), bottom)
        part[:, 0, :, at] = even.reshape(32, 8, width)
        part[:, 1, :, at] = odd.reshape(32, 8, width)

    def trade(at, i):
        send(part.at[pl.ds((1 - core) * 16, 16), :, :, at], sib.at[:, :, :, at], s_d2.at[i], r_d2.at[i], sibling)

    def collect(at, i):
        landed(sib.at[:, :, :, at], r_d2.at[i])

        @pl.loop(0, 16)
        def _(pair):
            row = core * 16 + pair
            part[row, :, :, at] = part[row, :, :, at] + sib[pair, :, :, at]

    sa, sb = pl.ds(0, SCUT), pl.ds(SCUT, SUMW - SCUT)

    def pa(dz, dx, at):
        xx = xat(dx)
        return part.at[core * 16 + zat(dz) * 2 + lax.div(xx, 2), lax.rem(xx, 2), :, at]

    def add(dst, src):
        dst[...] = dst[...] + src[...]

    def a_away(i):
        to = x_up if i % 2 == 0 else x_down
        send(pa(ORDER[i], 2, sa), ax_f.at[i], s_af.at[i], r_af.at[i], to)

    def a_near(i):
        if i % 2 == 0:
            send(pa(ORDER[i], -1, sa), ax_r.at[i], s_ar.at[i], r_ar.at[i], x_down)
        else:
            send(pa(ORDER[i], 1, sa), ax_l.at[i], s_al.at[i], r_al.at[i], x_up)

    def a_far(i):
        d = ORDER[i]
        landed(ax_f.at[i], r_af.at[i])
        if i % 2 == 0:
            add(ax_f.at[i], pa(d, 1, sa))
            send(ax_f.at[i], ax_l.at[i], s_al.at[i], r_al.at[i], x_up)
        else:
            add(ax_f.at[i], pa(d, -1, sa))
            send(ax_f.at[i], ax_r.at[i], s_ar.at[i], r_ar.at[i], x_down)

    def a_sum(i):
        own_ = pa(ORDER[i], 0, sa)
        landed(ax_l.at[i], r_al.at[i])
        landed(ax_r.at[i], r_ar.at[i])
        own_[...] = own_[...] + ax_l[i] + ax_r[i]
        if i < 3:
            send(own_, ae.at[i], s_ae.at[i], r_ae.at[i], device(y, core, x, zat((-2, -1, 1)[i])))
        elif i in (5, 6):
            send(own_, ag.at[i - 5], s_ag.at[i - 5], r_ag.at[i - 5], device(y, core, x, zat(ORDER[i])))

    def a_join():
        ref = pa(-2, 0, sa)
        landed(ae.at[0], r_ae.at[0])
        landed(ae.at[1], r_ae.at[1])
        ref[...] = ref[...] + ae[0] + ae[1]
        send(ref, ag.at[2], s_ag.at[2], r_ag.at[2], device(y, core, x, zat(-2)))
        ref = pa(2, 0, sa)
        landed(ae.at[2], r_ae.at[2])
        ref[...] = ref[...] + ae[2]
        send(ref, ag.at[3], s_ag.at[3], r_ag.at[3], device(y, core, x, zat(2)))

    def a_end():
        own_ = pa(0, 0, sa)
        for i in range(4):
            landed(ag.at[i], r_ag.at[i])
        own_[...] = own_[...] + ((ag[0] + ag[1]) + (ag[2] + ag[3]))

    def pb(dz):
        return part.at[pl.ds(core * 16 + zat(dz) * 2, 2), :, :, sb]

    def b_start():
        for i, (row, step) in enumerate(((4, 2), (3, 1), (-3, -1))):
            send(pb(row), be.at[i], s_be.at[i], r_be.at[i], device(y, core, x, zat(step)))
        for i, step in enumerate((-1, 1)):
            send(pb(step), bg.at[i], s_bg.at[i], r_bg.at[i], device(y, core, x, zat(step)))

    def b_join():
        landed(be.at[0], r_be.at[0])
        landed(be.at[1], r_be.at[1])
        ref = pb(2)
        ref[...] = ref[...] + be[0] + be[1]
        send(ref, bg.at[2], s_bg.at[2], r_bg.at[2], device(y, core, x, zat(2)))
        landed(be.at[2], r_be.at[2])
        ref = pb(-2)
        ref[...] = ref[...] + be[2]
        send(ref, bg.at[3], s_bg.at[3], r_bg.at[3], device(y, core, x, zat(-2)))

    def b_sum():
        for i in range(4):
            landed(bg.at[i], r_bg.at[i])
        ref = pb(0)
        ref[...] = ref[...] + ((bg[0] + bg[1]) + (bg[2] + bg[3]))
        for i in range(3):
            send(pa(0, XPEER[i], sb), bx.at[i], s_bx.at[i], r_bx.at[i], x_peers[i])

    def b_end():
        own_ = pa(0, 0, sb)
        for i in range(3):
            landed(bx.at[i], r_bx.at[i])
        own_[...] = own_[...] + bx[0] + (bx[1] + bx[2])

    def piece(start, width):
        store(
            pl.ds(128 + start, width), product(pl.ds(start, width)), product(pl.ds(FPIX + start, width)), width
        )

    cuts = [pl.ds(0, 640), pl.ds(640, 512), pl.ds(1152, 512)]
    piece(1536, 512)
    trade(sb, 3)
    edge = product(pl.ds(2 * FPIX, 128))
    store(pl.ds(0, 128), edge, edge, 128)
    piece(0, 512)
    trade(cuts[0], 0)
    piece(512, 512)
    trade(cuts[1], 1)
    collect(sb, 3)
    b_start()
    piece(1024, 512)
    trade(cuts[2], 2)
    for i in range(3):
        collect(cuts[i], i)
    for i in range(6):
        a_away(i)
    a_near(1)
    a_near(0)
    b_join()
    a_far(0)
    a_far(1)
    a_away(6)
    a_away(7)
    a_far(2)
    a_far(3)
    a_near(3)
    a_near(2)
    a_far(4)
    a_far(5)
    a_near(5)
    a_near(4)
    a_sum(0)
    a_sum(1)
    b_sum()
    a_far(6)
    a_far(7)
    a_near(7)
    a_near(6)
    a_sum(2)
    a_sum(3)
    a_sum(4)
    a_join()
    a_sum(5)
    a_sum(6)
    b_end()
    a_sum(7)
    a_end()

    done = part[core * 16 + z * 2 + lax.div(x, 2), lax.rem(x, 2)]
    pair = lax.broadcasted_iota(jnp.int32, (1, 2), 1)
    for r in range(2):
        counts_out[r] = jnp.where(pair == 0, done[2 * r : 2 * r + 1, 0:1], done[2 * r + 1 : 2 * r + 2, 0:1])
        for k in range(2):
            for c in range(2):
                row = 4 * c + 2 * r + k
                sums_out[r, k, c : c + 1, :] = done[row : row + 1, 128:SUMW]

    landed(llr.at[1 - core], r_ll)
    value = jnp.where(
        lax.broadcasted_iota(jnp.int32, (8, 128), 1) < 32,
        jnp.where(y_hi == 0, llr[0], pltpu.roll(llr[0], 96, 1)),
        jnp.where(y_hi == 1, llr[1], pltpu.roll(llr[1], 32, 1)),
    )
    loglik_out[0:1, :] = value[0:1, 0:64]
    loglik_out[1:2, :] = value[2:3, 0:64]

    left(pix.at[0], s_pix.at[0])
    left(offs.at[0], s_pix.at[1])
    left(llr.at[0], s_ll)
    for i in range(3):
        left(stats.at[0], s_st.at[i])
        left(gb(0, 0), s_y.at[i])
        left(be.at[0], s_be.at[i])
        left(ae.at[0], s_ae.at[i])
        left(bx.at[0], s_bx.at[i])
    for i in range(4):
        left(bg.at[0], s_bg.at[i])
        left(ag.at[0], s_ag.at[i])
    for i in range(7):
        left(ga(0, 0), s_z.at[i])
        left(gb_row(0), s_w.at[i])
    for i in range(8):
        for k in range(3):
            left(ga(0, 0), s_x.at[i, k])
        left(ga_row(0), s_sd.at[i])
        left(gb_row(0), s_se.at[i])
        left(ax_f.at[0], s_af.at[i])
        left(ax_f.at[0], s_al.at[i])
        left(ax_f.at[0], s_ar.at[i])
    for i in range(3):
        left(sib.at[:, :, :, cuts[i]], s_d2.at[i])
    left(sib.at[:, :, :, sb], s_d2.at[3])


def local(particles, offsets, ref_maps, inv_sigma2, log_prior, orient):
    f32, bf16 = jnp.float32, jnp.bfloat16
    vmem = pl.BlockSpec(memory_space=pltpu.VMEM)
    smem = pl.BlockSpec(memory_space=pltpu.SMEM)
    dma = pltpu.SemaphoreType.DMA

    def twice(*shape):
        return [dma(shape), dma(shape)] if shape else [dma, dma]

    rest = SUMW - SCUT
    scratch = [
        pltpu.VMEM((64, 2, FPIX), bf16),
        pltpu.VMEM((2, 64, 2, FPIX), bf16),
        pltpu.VMEM((16, PACK), f32),
        pltpu.VMEM((2, ZN, XN, 16, PACK), bf16),
        pltpu.VMEM((2, 2, HALF, FPIX), bf16),
        pltpu.VMEM((2, HALF, 128), jnp.int32),
        pltpu.VMEM((3, HALF, 128), f32),
        pltpu.VMEM((ROWS, WIDTH), bf16),
        pltpu.VMEM((256, WIDTH), bf16),
        pltpu.VMEM((256, ROWS), f32),
        pltpu.VMEM((256, ROWS), bf16),
        pltpu.VMEM((4, 2, 8, 128), f32),
        pltpu.VMEM((32, 2, 8, SUMW), f32),
        pltpu.VMEM((16, 2, 8, SUMW), f32),
        pltpu.VMEM((2, 8, 128), f32),
        pltpu.VMEM((8, 8, SCUT), f32),
        pltpu.VMEM((8, 8, SCUT), f32),
        pltpu.VMEM((8, 8, SCUT), f32),
        pltpu.VMEM((3, 8, SCUT), f32),
        pltpu.VMEM((4, 8, SCUT), f32),
        pltpu.VMEM((3, 2, 2, 8, rest), f32),
        pltpu.VMEM((4, 2, 2, 8, rest), f32),
        pltpu.VMEM((3, 8, rest), f32),
    ]
    scratch += [dma((2,))] + twice(2) + twice(3) + twice()
    scratch += twice(7) + twice(8, 3) + twice(8) + twice(3) + twice(7) + twice(8)
    scratch += twice(4) + twice(8) * 3 + twice(3) + twice(4)
    scratch += twice(3) + twice(4) + twice(3)
    hbm = pl.BlockSpec(memory_space=pl.ANY)
    sums, counts, loglik = pl.pallas_call(
        kernel,
        out_shape=(
            jax.ShapeDtypeStruct((2, 2, 2, FPIX), f32),
            jax.ShapeDtypeStruct((2, 1, 2), f32),
            jax.ShapeDtypeStruct((2, 64), f32),
        ),
        in_specs=[smem, smem, smem, vmem, vmem, hbm, hbm],
        out_specs=(vmem, vmem, vmem),
        scratch_shapes=scratch,
        compiler_params=pltpu.CompilerParams(
            collective_id=0, has_side_effects=True, vmem_limit_bytes=56 * 1024 * 1024
        ),
    )(orient.T, log_prior, offsets.T, inv_sigma2.reshape(1, FPIX), jnp.asarray(tables()), particles, ref_maps)
    return sums.reshape(2, 2, 1, 2, FPIX), counts.transpose(0, 2, 1), loglik


def solution(mesh):
    return jax.shard_map(
        local,
        mesh=mesh,
        in_specs=(
            P("dom", None, None),
            P("dom", None),
            P("cls", "dom", None, None),
            P(),
            P("cls"),
            P(None, "dom"),
        ),
        out_specs=(P(None, "cls", "dom", None, None), P(None, "cls", "dom"), P(None, "dom")),
        check_vma=False,
    )
```

time: 91.7 us -> 70.2 us (0.77)
  Pallas kernels: 85.1 us -> 66.6 us
  local copies, waits for them, and re-layouts: 5.13 us -> 2.7 us
    pallas_call x1, Pallas kernels: 85.1 us -> 66.6 us  [local(): pl.pallas_call(kernel, out_shape=(jax.ShapeDtypeStruct((2, 2, 2, FPIX), f...]
    reshape x2 -> x0, local copies, waits for them, and re-layouts: 1.56 us -> none  [local(): sums.reshape(2, 2, 2, FPIX).transpose(1, 2, 0, 3).reshape(2, 2, 1, 2, FPIX)]
    unnamed x6 -> x7, local copies, waits for them, and re-layouts: 2.04 us -> 2.7 us
where the time goes in v2:
time: 70.2 us; the launch traced here: 69.9 us
  Pallas kernels  66.6 us (95%)
  local copies, waits for them, and re-layouts  2.7 us (4%)
    pallas_call x1, Pallas kernels, local(): pl.pallas_call(kernel, out_shape=(jax.ShapeDtypeStruct((2, 2, 2, FPIX), f...  66.6 us
    unnamed x7, local copies, waits for them, and re-layouts  2.7 us

profile of v2, /device:TPU:1, one launch (start us, length us, event | category | flops | bytes accessed | tf_op | source)
XLA Modules:
  0.0 69.9 jit_solution(12156203110208030135)
XLA Ops:
  0.6 66.6 %shard_map.94 = (f32[2,2,2,2048]{3,2,1,0:T(2,128)}, f32[2,1,2]{2,1,0:T(1,128)}, f32[2,64]{1,0:T(2,128)}) custom-call(s32[1,2]{1,0:T(1,128)} %bitcast.13, f32[2]{0:T(128)} %prior.1, s32[2,64]{1,0:T(2,128)} %bitcast.11, f32[1,2048]{1,0:T(1,128)} %bitcast.10, f32[17,8,128]{2,1,0:T(8,128)} %constant.2.clone.table, bf16[64,2,2048]{2,1,0:T(2,128)(2,1)} %particles_hbm.1, ...), custom_call_target="tpu_custom_call" | custom-call | tf_op jit(solution)/shard_map/pallas_call | solution.py:603
  67.2 0.0 copy-start.1
  67.2 1.5 %copy.15 = f32[2,2,1,2,2048]{4,3,2,1,0:T(2,128)} copy(f32[2,2,1,2,2048]{4,3,2,1,0:T(2,128)} %bitcast.9) | data formatting | bytes 131072
  68.7 0.0 copy-done.1
  68.7 0.0 copy-start
  68.7 0.6 copy.16
  69.3 0.1 copy-done
  69.4 0.6 copy.17
Async XLA Ops:
  67.2 1.5 %copy-start.1 = (f32[2,1,2]{2,1,0:T(1,128)S(1)}, f32[2,1,2]{2,1,0:T(1,128)}, u32[]{:S(2)}) copy-start(f32[2,1,2]{2,1,0:T(1,128)} %get-tuple-element.7) | copy-start | bytes 52
  68.7 0.7 copy-start

commit v3 on v2

--- a/solution.py
+++ b/solution.py
@@ -256,45 +256,76 @@
     w(6, 2, -1)
     from_w(2, -1, 1)
     from_w(3, 1, 2)
+    def spread(c, j, begin, end):
+        width = end - begin
+        rows = pl.ds(pl.multiple_of((c * 8 + zat(DELTA[j])) * 16, 16), 16)
+        upper = lax.broadcasted_iota(jnp.int32, (8, width), 0) < 4
+        tiles = [gath[c, zat(DELTA[j]), i, :, begin:end].astype(jnp.float32) for i in range(4)]
+        for t in range(2):
+            t0, t1, t2, t3 = [tile[8 * t : 8 * t + 8] for tile in tiles]
+            place = 2048 * t + begin if begin < 1024 else 2 * FPIX
+            weights[rows, place : place + width] = jnp.concatenate(
+                [jnp.where(upper, t0, pltpu.roll(t1, 4, 0)), jnp.where(upper, t2, pltpu.roll(t3, 4, 0))], axis=0
+            ).astype(jnp.bfloat16)
+            if begin == 1024:
+                break
+            place = 2048 * t + 1024 + begin
+            weights[rows, place : place + width] = jnp.concatenate(
+                [jnp.where(upper, pltpu.roll(t0, 4, 0), t1), jnp.where(upper, pltpu.roll(t2, 4, 0), t3)], axis=0
+            ).astype(jnp.bfloat16)
+
+    def own_a(*which):
+        for j in which:
+            spread(core, j, 0, GCUT)
+
+    def own_b(*which):
+        for j in which:
+            spread(core, j, GCUT, 1024)
+            spread(core, j, 1024, PACK)
+
+    def sib_a(*which):
+        for j in which:
+            landed(ga_row(DELTA[j], 1 - core), r_sd.at[j])
+            spread(1 - core, j, 0, GCUT)
+
+    def sib_b(*which):
+        for j in which:
+            landed(gb_row(DELTA[j], 1 - core), r_se.at[j])
+            spread(1 - core, j, GCUT, 1024)
+            spread(1 - core, j, 1024, PACK)
+
     row_a(2)
+    own_a(0, 1)
+    own_b(0)
+    sib_a(0)
+    sib_b(0)
     landed(offs.at[1 - y_hi], r_pix.at[1])
     landed(pix.at[1 - y_hi], r_pix.at[0])
     prepare(1 - y_hi)
-    shift(1 - y_hi, 0, 6)
+    shift(1 - y_hi, 0, 8)
     row_a(3)
     row_a(4)
-    shift(1 - y_hi, 6, 12)
+    own_a(2)
+    own_b(1, 2, 3, 4)
+    shift(1 - y_hi, 8, 16)
     row_a(5)
     row_a(6)
+    own_a(3, 4)
+    sib_a(1, 2)
+    sib_b(1, 2, 3, 4)
     from_w(4, -3, 5)
     from_w(6, 3, 6)
-    shift(1 - y_hi, 12, 16)
+    own_a(5, 6)
+    own_b(5, 6)
+    sib_a(3, 4)
     from_w(5, -4, 7)
     row_a(7)
-    for j in range(8):
-        landed(ga_row(DELTA[j], 1 - core), r_sd.at[j])
-        landed(gb_row(DELTA[j], 1 - core), r_se.at[j])
-
-    upper = lax.broadcasted_iota(jnp.int32, (8, 1024), 0) < 4
-
-    @pl.loop(0, 16)
-    def _(group):
-        gb_, gz = lax.div(group, 8), lax.rem(group, 8)
-        rows = pl.ds(pl.multiple_of(group * 16, 16), 16)
-        tiles = [gath[gb_, gz, i].astype(jnp.float32) for i in range(4)]
-        for t in range(2):
-            t0, t1, t2, t3 = [tile[8 * t : 8 * t + 8, 0:1024] for tile in tiles]
-            weights[rows, 2048 * t : 2048 * t + 1024] = jnp.concatenate(
-                [jnp.where(upper, t0, pltpu.roll(t1, 4, 0)), jnp.where(upper, t2, pltpu.roll(t3, 4, 0))], axis=0
-            ).astype(jnp.bfloat16)
-            weights[rows, 2048 * t + 1024 : 2048 * t + 2048] = jnp.concatenate(
-                [jnp.where(upper, pltpu.roll(t0, 4, 0), t1), jnp.where(upper, pltpu.roll(t2, 4, 0), t3)], axis=0
-            ).astype(jnp.bfloat16)
-        t0, t1, t2, t3 = [tile[0:8, 1024:PACK] for tile in tiles]
-        up = upper[:, 0:128]
-        weights[rows, 2 * FPIX : WIDTH] = jnp.concatenate(
-            [jnp.where(up, t0, pltpu.roll(t1, 4, 0)), jnp.where(up, t2, pltpu.roll(t3, 4, 0))], axis=0
-        ).astype(jnp.bfloat16)
+    own_a(7)
+    own_b(7)
+    sib_a(5, 6)
+    sib_b(5, 6)
+    sib_a(7)
+    sib_b(7)
 
     @pl.loop(0, 2)
     def _(tile):
@@ -379,52 +410,64 @@
     def add(dst, src):
         dst[...] = dst[...] + src[...]
 
-    def a_away(i):
+    acols = [pl.ds(0, 896), pl.ds(896, 768)]
+    acut = [pl.ds(0, 896), pl.ds(0, 768)]
+
+    def a_away(p, i):
         to = x_up if i % 2 == 0 else x_down
-        send(pa(ORDER[i], 2, sa), ax_f.at[i], s_af.at[i], r_af.at[i], to)
-
-    def a_near(i):
+        send(pa(ORDER[i], 2, acols[p]), ax_f.at[p, i, :, acut[p]], s_af.at[p, i], r_af.at[p, i], to)
+
+    def a_near(p, i):
         if i % 2 == 0:
-            send(pa(ORDER[i], -1, sa), ax_r.at[i], s_ar.at[i], r_ar.at[i], x_down)
+            send(pa(ORDER[i], -1, acols[p]), ax_r.at[p, i, :, acut[p]], s_ar.at[p, i], r_ar.at[p, i], x_down)
         else:
-            send(pa(ORDER[i], 1, sa), ax_l.at[i], s_al.at[i], r_al.at[i], x_up)
-
-    def a_far(i):
+            send(pa(ORDER[i], 1, acols[p]), ax_l.at[p, i, :, acut[p]], s_al.at[p, i], r_al.at[p, i], x_up)
+
+    def a_far(p, i):
         d = ORDER[i]
-        landed(ax_f.at[i], r_af.at[i])
+        landed(ax_f.at[p, i, :, acut[p]], r_af.at[p, i])
         if i % 2 == 0:
-            add(ax_f.at[i], pa(d, 1, sa))
-            send(ax_f.at[i], ax_l.at[i], s_al.at[i], r_al.at[i], x_up)
+            add(ax_f.at[p, i, :, acut[p]], pa(d, 1, acols[p]))
+            send(ax_f.at[p, i, :, acut[p]], ax_l.at[p, i, :, acut[p]], s_al.at[p, i], r_al.at[p, i], x_up)
         else:
-            add(ax_f.at[i], pa(d, -1, sa))
-            send(ax_f.at[i], ax_r.at[i], s_ar.at[i], r_ar.at[i], x_down)
-
-    def a_sum(i):
-        own_ = pa(ORDER[i], 0, sa)
-        landed(ax_l.at[i], r_al.at[i])
-        landed(ax_r.at[i], r_ar.at[i])
-        own_[...] = own_[...] + ax_l[i] + ax_r[i]
-        if i < 3:
-            send(own_, ae.at[i], s_ae.at[i], r_ae.at[i], device(y, core, x, zat((-2, -1, 1)[i])))
+            add(ax_f.at[p, i, :, acut[p]], pa(d, -1, acols[p]))
+            send(ax_f.at[p, i, :, acut[p]], ax_r.at[p, i, :, acut[p]], s_ar.at[p, i], r_ar.at[p, i], x_down)
+
+    def a_sum(p, i):
+        own_ = pa(ORDER[i], 0, acols[p])
+        landed(ax_l.at[p, i, :, acut[p]], r_al.at[p, i])
+        landed(ax_r.at[p, i, :, acut[p]], r_ar.at[p, i])
+        own_[...] = own_[...] + ax_l[p, i, :, acut[p]] + ax_r[p, i, :, acut[p]]
+        if p == 1 and i in (0, 1, 2):
+            send(own_, ae.at[p, i, :, acut[p]], s_ae.at[p, i], r_ae.at[p, i], device(y, core, x, zat(ORDER[i])))
+        elif p == 1 and i in (3, 4):
+            k = i - 1
+            send(own_, ag.at[p, k, :, acut[p]], s_ag.at[p, k], r_ag.at[p, k], device(y, core, x, zat(ORDER[i])))
+        elif i < 3:
+            send(own_, ae.at[p, i, :, acut[p]], s_ae.at[p, i], r_ae.at[p, i], device(y, core, x, zat((-2, -1, 1)[i])))
         elif i in (5, 6):
-            send(own_, ag.at[i - 5], s_ag.at[i - 5], r_ag.at[i - 5], device(y, core, x, zat(ORDER[i])))
-
-    def a_join():
-        ref = pa(-2, 0, sa)
-        landed(ae.at[0], r_ae.at[0])
-        landed(ae.at[1], r_ae.at[1])
-        ref[...] = ref[...] + ae[0] + ae[1]
-        send(ref, ag.at[2], s_ag.at[2], r_ag.at[2], device(y, core, x, zat(-2)))
-        ref = pa(2, 0, sa)
-        landed(ae.at[2], r_ae.at[2])
-        ref[...] = ref[...] + ae[2]
-        send(ref, ag.at[3], s_ag.at[3], r_ag.at[3], device(y, core, x, zat(2)))
-
-    def a_end():
-        own_ = pa(0, 0, sa)
+            send(own_, ag.at[p, i - 5, :, acut[p]], s_ag.at[p, i - 5], r_ag.at[p, i - 5], device(y, core, x, zat(ORDER[i])))
+
+    def a_join(p):
+        ref = pa(-2, 0, acols[p])
+        landed(ae.at[p, 0, :, acut[p]], r_ae.at[p, 0])
+        landed(ae.at[p, 1, :, acut[p]], r_ae.at[p, 1])
+        ref[...] = ref[...] + ae[p, 0, :, acut[p]] + ae[p, 1, :, acut[p]]
+        send(ref, ag.at[p, 2, :, acut[p]], s_ag.at[p, 2], r_ag.at[p, 2], device(y, core, x, zat(-2)))
+        ref = pa(2, 0, acols[p])
+        landed(ae.at[p, 2, :, acut[p]], r_ae.at[p, 2])
+        ref[...] = ref[...] + ae[p, 2, :, acut[p]]
+        send(ref, ag.at[p, 3, :, acut[p]], s_ag.at[p, 3], r_ag.at[p, 3], device(y, core, x, zat(2)))
+
+    def a_end(p):
+        own_ = pa(0, 0, acols[p])
+        if p == 1:
+            for i in range(3):
+                landed(ae.at[p, i, :, acut[p]], r_ae.at[p, i])
+            own_[...] = own_[...] + ae[p, 0, :, acut[p]] + (ae[p, 1, :, acut[p]] + ae[p, 2, :, acut[p]])
         for i in range(4):
-            landed(ag.at[i], r_ag.at[i])
-        own_[...] = own_[...] + ((ag[0] + ag[1]) + (ag[2] + ag[3]))
+            landed(ag.at[p, i, :, acut[p]], r_ag.at[p, i])
+        own_[...] = own_[...] + ((ag[p, 0, :, acut[p]] + ag[p, 1, :, acut[p]]) + (ag[p, 2, :, acut[p]] + ag[p, 3, :, acut[p]]))
 
     def pb(dz):
         return part.at[pl.ds(core * 16 + zat(dz) * 2, 2), :, :, sb]
@@ -465,54 +508,69 @@
             pl.ds(128 + start, width), product(pl.ds(start, width)), product(pl.ds(FPIX + start, width)), width
         )
 
-    cuts = [pl.ds(0, 640), pl.ds(640, 512), pl.ds(1152, 512)]
-    piece(1536, 512)
-    trade(sb, 3)
     edge = product(pl.ds(2 * FPIX, 128))
     store(pl.ds(0, 128), edge, edge, 128)
     piece(0, 512)
-    trade(cuts[0], 0)
-    piece(512, 512)
-    trade(cuts[1], 1)
-    collect(sb, 3)
+    piece(512, 256)
+    trade(acols[0], 0)
+    piece(1536, 512)
+    trade(sb, 2)
+    collect(acols[0], 0)
+    for i in range(8):
+        a_away(0, i)
+    for i in (1, 0, 3, 2):
+        a_near(0, i)
+    piece(768, 512)
+    collect(sb, 2)
     b_start()
-    piece(1024, 512)
-    trade(cuts[2], 2)
+    a_far(0, 0)
+    a_far(0, 1)
+    piece(1280, 256)
+    trade(acols[1], 1)
+    a_far(0, 2)
+    a_far(0, 3)
+    a_near(0, 5)
+    a_near(0, 4)
+    a_far(0, 4)
+    a_far(0, 5)
+    a_near(0, 7)
+    a_near(0, 6)
+    a_far(0, 6)
+    a_far(0, 7)
+    collect(acols[1], 1)
+    for i in range(8):
+        a_away(1, i)
+    for i in (1, 0, 3, 2):
+        a_near(1, i)
     for i in range(3):
-        collect(cuts[i], i)
-    for i in range(6):
-        a_away(i)
-    a_near(1)
-    a_near(0)
+        a_sum(0, i)
     b_join()
-    a_far(0)
-    a_far(1)
-    a_away(6)
-    a_away(7)
-    a_far(2)
-    a_far(3)
-    a_near(3)
-    a_near(2)
-    a_far(4)
-    a_far(5)
-    a_near(5)
-    a_near(4)
-    a_sum(0)
-    a_sum(1)
+    a_far(1, 0)
+    a_far(1, 1)
+    a_sum(0, 3)
+    a_sum(0, 4)
+    a_far(1, 2)
+    a_far(1, 3)
+    a_near(1, 5)
+    a_near(1, 4)
+    a_far(1, 4)
+    a_far(1, 5)
+    a_near(1, 7)
+    a_near(1, 6)
+    a_sum(0, 5)
+    a_sum(0, 6)
+    a_join(0)
+    a_far(1, 6)
+    a_far(1, 7)
     b_sum()
-    a_far(6)
-    a_far(7)
-    a_near(7)
-    a_near(6)
-    a_sum(2)
-    a_sum(3)
-    a_sum(4)
-    a_join()
-    a_sum(5)
-    a_sum(6)
+    for i in range(5):
+        a_sum(1, i)
+    for i in range(5, 8):
+        a_sum(1, i)
+    a_sum(0, 7)
     b_end()
-    a_sum(7)
-    a_end()
+    a_end(0)
+    a_end(1)
 
     done = part[core * 16 + z * 2 + lax.div(x, 2), lax.rem(x, 2)]
     pair = lax.broadcasted_iota(jnp.int32, (1, 2), 1)
@@ -539,11 +597,9 @@
         left(stats.at[0], s_st.at[i])
         left(gb(0, 0), s_y.at[i])
         left(be.at[0], s_be.at[i])
-        left(ae.at[0], s_ae.at[i])
         left(bx.at[0], s_bx.at[i])
     for i in range(4):
         left(bg.at[0], s_bg.at[i])
-        left(ag.at[0], s_ag.at[i])
     for i in range(7):
         left(ga(0, 0), s_z.at[i])
         left(gb_row(0), s_w.at[i])
@@ -552,12 +608,17 @@
             left(ga(0, 0), s_x.at[i, k])
         left(ga_row(0), s_sd.at[i])
         left(gb_row(0), s_se.at[i])
-        left(ax_f.at[0], s_af.at[i])
-        left(ax_f.at[0], s_al.at[i])
-        left(ax_f.at[0], s_ar.at[i])
-    for i in range(3):
-        left(sib.at[:, :, :, cuts[i]], s_d2.at[i])
-    left(sib.at[:, :, :, sb], s_d2.at[3])
+    for p in range(2):
+        for i in range(8):
+            left(ax_f.at[p, 0, :, acut[p]], s_af.at[p, i])
+            left(ax_f.at[p, 0, :, acut[p]], s_al.at[p, i])
+            left(ax_f.at[p, 0, :, acut[p]], s_ar.at[p, i])
+        for i in range(3):
+            left(ae.at[p, 0, :, acut[p]], s_ae.at[p, i])
+        for i in range(4):
+            left(ag.at[p, 0, :, acut[p]], s_ag.at[p, i])
+        left(sib.at[:, :, :, acols[p]], s_d2.at[p])
+    left(sib.at[:, :, :, sb], s_d2.at[2])
 
 
 def local(particles, offsets, ref_maps, inv_sigma2, log_prior, orient):
@@ -586,18 +647,18 @@
         pltpu.VMEM((32, 2, 8, SUMW), f32),
         pltpu.VMEM((16, 2, 8, SUMW), f32),
         pltpu.VMEM((2, 8, 128), f32),
-        pltpu.VMEM((8, 8, SCUT), f32),
-        pltpu.VMEM((8, 8, SCUT), f32),
-        pltpu.VMEM((8, 8, SCUT), f32),
-        pltpu.VMEM((3, 8, SCUT), f32),
-        pltpu.VMEM((4, 8, SCUT), f32),
+        pltpu.VMEM((2, 8, 8, 896), f32),
+        pltpu.VMEM((2, 8, 8, 896), f32),
+        pltpu.VMEM((2, 8, 8, 896), f32),
+        pltpu.VMEM((2, 3, 8, 896), f32),
+        pltpu.VMEM((2, 4, 8, 896), f32),
         pltpu.VMEM((3, 2, 2, 8, rest), f32),
         pltpu.VMEM((4, 2, 2, 8, rest), f32),
         pltpu.VMEM((3, 8, rest), f32),
     ]
     scratch += [dma((2,))] + twice(2) + twice(3) + twice()
     scratch += twice(7) + twice(8, 3) + twice(8) + twice(3) + twice(7) + twice(8)
-    scratch += twice(4) + twice(8) * 3 + twice(3) + twice(4)
+    scratch += twice(3) + twice(2, 8) * 3 + twice(2, 3) + twice(2, 4)
     scratch += twice(3) + twice(4) + twice(3)
     hbm = pl.BlockSpec(memory_space=pl.ANY)
     sums, counts, loglik = pl.pallas_call(

time: 70.2 us -> 68.3 us (0.973)
  Pallas kernels: 66.6 us -> 64.8 us
    pallas_call x1, Pallas kernels: 66.6 us -> 64.8 us  [local(): pl.pallas_call(kernel, out_shape=(jax.ShapeDtypeStruct((2, 2, 2, FPIX), f...]
where the time goes in v3:
time: 68.3 us; the launch traced here: 68.1 us
  Pallas kernels  64.8 us (95%)
  local copies, waits for them, and re-layouts  2.7 us (4%)
    pallas_call x1, Pallas kernels, local(): pl.pallas_call(kernel, out_shape=(jax.ShapeDtypeStruct((2, 2, 2, FPIX), f...  64.8 us
    unnamed x7, local copies, waits for them, and re-layouts  2.7 us

profile of v3, /device:TPU:1, one launch (start us, length us, event | category | flops | bytes accessed | tf_op | source)
XLA Modules:
  0.0 68.1 jit_solution(4558109055223594038)
XLA Ops:
  0.6 64.8 %shard_map.94 = (f32[2,2,2,2048]{3,2,1,0:T(2,128)}, f32[2,1,2]{2,1,0:T(1,128)}, f32[2,64]{1,0:T(2,128)}) custom-call(s32[1,2]{1,0:T(1,128)} %bitcast.13, f32[2]{0:T(128)} %prior.1, s32[2,64]{1,0:T(2,128)} %bitcast.11, f32[1,2048]{1,0:T(1,128)} %bitcast.10, f32[17,8,128]{2,1,0:T(8,128)} %constant.2.clone.table, bf16[64,2,2048]{2,1,0:T(2,128)(2,1)} %particles_hbm.1, ...), custom_call_target="tpu_custom_call" | custom-call | tf_op jit(solution)/shard_map/pallas_call | solution.py:664
  65.4 0.0 copy-start.1
  65.4 1.5 %copy.15 = f32[2,2,1,2,2048]{4,3,2,1,0:T(2,128)} copy(f32[2,2,1,2,2048]{4,3,2,1,0:T(2,128)} %bitcast.9) | data formatting | bytes 131072
  66.9 0.0 copy-done.1
  66.9 0.0 copy-start
  66.9 0.6 copy.16
  67.5 0.1 copy-done
  67.6 0.6 copy.17
Async XLA Ops:
  65.4 1.5 %copy-start.1 = (f32[2,1,2]{2,1,0:T(1,128)S(1)}, f32[2,1,2]{2,1,0:T(1,128)}, u32[]{:S(2)}) copy-start(f32[2,1,2]{2,1,0:T(1,128)} %get-tuple-element.7) | copy-start | bytes 52
  66.9 0.7 copy-start

commit v4 on v3

--- a/solution.py
+++ b/solution.py
@@ -25,6 +25,7 @@
 SCUT = 1664
 DELTA = (0, -1, 1, -2, 2, -3, 3, -4)
 XPEER = (1, -1, 2)
+YPEER = (2, 1, 3)
 ZPEER = (1, -1, 2, -2, 3, -3, 4)
 ORDER = (4, -3, 3, -2, 2, -1, 1, 0)
 
@@ -67,7 +68,7 @@
 
 def kernel(
     orient, prior, offsets, noise, table, particles_hbm, maps_hbm,
-    sums_out, counts_out, loglik_out,
+    sums_out, rest_out,
     particles, maps, block, gath, pix, offs, base, shifted, weights, logits, post, stats,
     part, sib, llr, ax_l, ax_r, ax_f, ae, ag, be, bg, bx,
     s_in, s_pix, r_pix, s_st, r_st, s_ll, r_ll,
@@ -97,7 +98,7 @@
     mate = device(3 - y, core, x, z)
     x_peers = [device(y, core, xat(d), z) for d in XPEER]
     z_peers = [device(y, core, x, zat(d)) for d in ZPEER]
-    y_peers = [device(yat(d), core, x, z) for d in (1, 2, 3)]
+    y_peers = [device(yat(d), core, x, z) for d in YPEER]
 
     def send(src, dst, ssem, rsem, to):
         copy = pltpu.make_async_remote_copy(
@@ -364,7 +365,7 @@
     for i in range(3):
         send(stats.at[y], stats.at[y], s_st.at[i], r_st.at[i], y_peers[i])
     for i in range(3):
-        landed(stats.at[yat(3 - i)], r_st.at[i])
+        landed(stats.at[yat(4 - YPEER[i])], r_st.at[i])
     peaks = [stats[i, 0] for i in range(4)]
     top = jnp.maximum(jnp.maximum(peaks[0], peaks[1]), jnp.maximum(peaks[2], peaks[3]))
     whole = stats[0, 1] * jnp.exp(peaks[0] - top)
@@ -573,13 +574,11 @@
     a_end(1)
 
     done = part[core * 16 + z * 2 + lax.div(x, 2), lax.rem(x, 2)]
-    pair = lax.broadcasted_iota(jnp.int32, (1, 2), 1)
     for r in range(2):
-        counts_out[r] = jnp.where(pair == 0, done[2 * r : 2 * r + 1, 0:1], done[2 * r + 1 : 2 * r + 2, 0:1])
         for k in range(2):
             for c in range(2):
-                row = 4 * c + 2 * r + k
-                sums_out[r, k, c : c + 1, :] = done[row : row + 1, 128:SUMW]
+                row, to = 4 * c + 2 * r + k, 4 * r + 2 * k + c
+                sums_out[to : to + 1, :] = done[row : row + 1, 128:SUMW]
 
     landed(llr.at[1 - core], r_ll)
     value = jnp.where(
@@ -587,8 +586,10 @@
         jnp.where(y_hi == 0, llr[0], pltpu.roll(llr[0], 96, 1)),
         jnp.where(y_hi == 1, llr[1], pltpu.roll(llr[1], 32, 1)),
     )
-    loglik_out[0:1, :] = value[0:1, 0:64]
-    loglik_out[1:2, :] = value[2:3, 0:64]
+    rest_out[0:1, :] = value[0:1]
+    rest_out[1:2, :] = value[2:3]
+    for r in range(2):
+        rest_out[2 + r : 3 + r, :] = jnp.where(lane == 0, done[2 * r : 2 * r + 1, 0:1], done[2 * r + 1 : 2 * r + 2, 0:1])
 
     left(pix.at[0], s_pix.at[0])
     left(offs.at[0], s_pix.at[1])
@@ -661,21 +662,20 @@
     scratch += twice(3) + twice(2, 8) * 3 + twice(2, 3) + twice(2, 4)
     scratch += twice(3) + twice(4) + twice(3)
     hbm = pl.BlockSpec(memory_space=pl.ANY)
-    sums, counts, loglik = pl.pallas_call(
+    sums, small = pl.pallas_call(
         kernel,
         out_shape=(
-            jax.ShapeDtypeStruct((2, 2, 2, FPIX), f32),
-            jax.ShapeDtypeStruct((2, 1, 2), f32),
-            jax.ShapeDtypeStruct((2, 64), f32),
+            jax.ShapeDtypeStruct((8, FPIX), f32),
+            jax.ShapeDtypeStruct((4, 128), f32),
         ),
         in_specs=[smem, smem, smem, vmem, vmem, hbm, hbm],
-        out_specs=(vmem, vmem, vmem),
+        out_specs=(vmem, vmem),
         scratch_shapes=scratch,
         compiler_params=pltpu.CompilerParams(
             collective_id=0, has_side_effects=True, vmem_limit_bytes=56 * 1024 * 1024
         ),
     )(orient.T, log_prior, offsets.T, inv_sigma2.reshape(1, FPIX), jnp.asarray(tables()), particles, ref_maps)
-    return sums.reshape(2, 2, 1, 2, FPIX), counts.transpose(0, 2, 1), loglik
+    return sums.reshape(2, 2, 1, 2, FPIX), small[2:4, 0:2].reshape(2, 2, 1), small[0:2, 0:64]
 
 
 def solution(mesh):

time: 68.3 us -> 68.4 us (level)
    unnamed x7 -> x2, local copies, waits for them, and re-layouts: 2.7 us -> 0.01 us
    reshape x0 -> x1, local copies, waits for them, and re-layouts: none -> 1.51 us  [local(): sums.reshape(2, 2, 1, 2, FPIX)]
    slice x0 -> x2, local copies, waits for them, and re-layouts: none -> 1.13 us  [the longest x1 0.56 us: local(): small[2:4, 0:2].reshape(2, 2, 1)]
where the time goes in v4:
time: 68.4 us; the launch traced here: 68.2 us
  Pallas kernels  64.9 us (95%)
  local copies, waits for them, and re-layouts  2.64 us (4%)
    pallas_call x1, Pallas kernels, local(): pl.pallas_call(kernel, out_shape=(jax.ShapeDtypeStruct((8, FPIX), f32), j...  64.9 us
    reshape x1, local copies, waits for them, and re-layouts, local(): sums.reshape(2, 2, 1, 2, FPIX)  1.51 us

profile of v4, /device:TPU:1, one launch (start us, length us, event | category | flops | bytes accessed | tf_op | source)
XLA Modules:
  0.0 68.2 jit_solution(16979661259543062916)
XLA Ops:
  0.6 64.9 %shard_map.94 = (f32[8,2048]{1,0:T(8,128)}, f32[4,128]{1,0:T(4,128)}) custom-call(s32[1,2]{1,0:T(1,128)} %bitcast.11, f32[2]{0:T(128)} %prior.1, s32[2,64]{1,0:T(2,128)} %bitcast.9, f32[1,2048]{1,0:T(1,128)} %bitcast.8, f32[17,8,128]{2,1,0:T(8,128)} %constant.2.clone.table, bf16[64,2,2048]{2,1,0:T(2,128)(2,1)} %particles_hbm.1, bf16[2,64,2,2048]{3,2,1,0:T(2,128)(2,1)} %maps_hbm.1), custom_call_target="tpu_custom_call" | custom-call | tf_op jit(solution)/shard_map/pallas_call | solution.py:665
  65.6 0.0 copy-start
  65.6 1.5 %reshape.16 = f32[2,2,1,2,2048]{4,3,1,0,2:T(2,128)} reshape(f32[8,2048]{1,0:T(8,128)} %get-tuple-element.5) | data formatting | bytes 131072 | tf_op jit(solution)/shard_map/reshape | solution.py:678
  67.1 0.0 copy-done
  67.1 0.6 slice.7
  67.7 0.6 slice.6
Async XLA Ops:
  65.6 1.5 %copy-start = (f32[4,128]{1,0:T(4,128)S(1)}, f32[4,128]{1,0:T(4,128)}, u32[]{:S(2)}) copy-start(f32[4,128]{1,0:T(4,128)} %get-tuple-element.6) | copy-start | bytes 6148
